TPU v7x, 256 devices: a whole 4x4x8 slice. The times are simulated.
256 devices in a mesh: seq: 64 (over z, y, core), mp: 4 (over x).
Axes of the slice: x: 4, y: 4, z: 8, core: 2. Of those that a mesh axis runs over, the one named last changes fastest.
Arguments:
- hidden: bfloat16 [65536, 4096], P('seq', 'mp')
- picked: int32 [8192], P('seq'), may hold values from 0 to 65535, as said below
- target: int32 [65536], P('seq'), may hold values from -1 to 8191, as said below
- norm_gain: bfloat16 [4096], replicated, may hold values from 0.099609375 to 1.8984375
- router_weight: bfloat16 [4096], replicated, may hold values from -0.1875 to 0.1875
- w_query: bfloat16 [4096, 2048], P('seq', 'mp')
- w_key: bfloat16 [4096, 2048], P('seq', 'mp')
- w_value: bfloat16 [4096, 2048], P('seq', 'mp'), may hold values from -0.1875 to 0.1875
- w_out: bfloat16 [2048, 4096], P(None, 'mp'), may hold values from -0.125 to 0.125
Outputs:
- mixed: bfloat16 [65536, 4096], P('seq', 'mp')
Inputs may be any that keep to these rules, and one draw needn't show every extreme that they name: `picked`: entry g holds the position of the routed token of rank (g mod 128) * 64 + g div 128, ranks counting the 8192 routed positions in increasing order. target[p] = g where picked[g] = p, and -1 where p is not routed; each aligned block of 1024 positions holds at most 256 routed ones, and some block holds exactly 256.
All inputs are finite; a program needn't handle non-finite values.
Results may differ from a plain program's by a relative error of at most 0.004.
Values may be sent and summed in bfloat16 or wider, within the bound.
No kernel may reach another device: no remote copies, remote signals or barrier semaphores. Data moves between devices by JAX's collectives and lax.ppermute only.
A program may use at most 128 MiB of HBM per device.

v0:
```python
import math

import jax
import jax.numpy as jnp
from jax import lax
from jax.sharding import PartitionSpec as P

HEAD_DIM = 128


def rotate(vec, positions):
    half = vec.shape[-1] // 2
    freq = jnp.exp(-math.log(10000.0) * (2.0 * jnp.arange(half, dtype=jnp.float32) / vec.shape[-1]))
    angle = positions.astype(jnp.float32)[:, None] * freq[None, :]
    cosine = jnp.cos(angle)[:, None, :]
    sine = jnp.sin(angle)[:, None, :]
    first = vec[..., :half]
    second = vec[..., half:]
    return jnp.concatenate(
        [first * cosine - second * sine, second * cosine + first * sine], axis=-1
    )


def per_device(hidden, picked, target, norm_gain, router_weight, w_query, w_key, w_value, w_out):
    shards = lax.axis_size("seq")
    here = lax.axis_index("seq")
    tok_rows = hidden.shape[0]
    part_width = hidden.shape[1]
    sel_rows = picked.shape[0]
    bucket = (2 * sel_rows + shards - 1) // shards
    live = target >= 0
    dest = jnp.where(live, target // sel_rows, shards)
    cell = dest * bucket + jnp.where(live, target % sel_rows, 0) % bucket
    table = jnp.full((shards * bucket,), tok_rows, jnp.int32)
    table = table.at[cell].set(jnp.arange(tok_rows, dtype=jnp.int32), mode="drop")
    padded = jnp.concatenate([hidden, jnp.zeros((1, part_width), hidden.dtype)], axis=0)
    outgoing = padded[table].reshape(shards, bucket, part_width)
    slots = jnp.arange(sel_rows, dtype=jnp.int32)
    source = picked // tok_rows
    fetch = source * bucket + slots % bucket
    arrived = lax.all_to_all(outgoing, "seq", split_axis=0, concat_axis=0, tiled=True)
    own_rows = arrived.reshape(shards * bucket, part_width)[fetch]
    full_rows = lax.all_gather(own_rows, "mp", axis=1, tiled=True)
    whole = full_rows.astype(jnp.float32)
    inverse = lax.rsqrt(jnp.mean(whole * whole, axis=-1, keepdims=True) + 1e-05)
    normed = (whole * inverse * norm_gain.astype(jnp.float32)).astype(jnp.bfloat16)
    gate = jax.nn.sigmoid(jnp.dot(full_rows, router_weight, preferred_element_type=jnp.float32))

    def add_rows(piece):
        return jnp.dot(normed, piece, preferred_element_type=jnp.float32)

    query_raw = add_rows(lax.all_gather(w_query, "seq", axis=0, tiled=True))
    key_raw = add_rows(lax.all_gather(w_key, "seq", axis=0, tiled=True))
    value_raw = add_rows(lax.all_gather(w_value, "seq", axis=0, tiled=True))
    heads = w_query.shape[1] // HEAD_DIM
    query = rotate(query_raw.reshape(sel_rows, heads, HEAD_DIM), picked).astype(jnp.bfloat16)
    keys = rotate(key_raw.reshape(sel_rows, heads, HEAD_DIM), picked).astype(jnp.bfloat16)
    values = value_raw.reshape(sel_rows, heads, HEAD_DIM).astype(jnp.bfloat16)
    rank_q = slots * shards + here
    scale = 1.0 / math.sqrt(HEAD_DIM)
    top = jnp.full((heads, sel_rows), -1e30, jnp.float32)
    piece_k = lax.all_gather(keys, "seq", axis=0, tiled=True)
    piece_v = lax.all_gather(values, "seq", axis=0, tiled=True)
    index = jnp.arange(piece_k.shape[0], dtype=jnp.int32)
    rank_k = index % sel_rows * shards + index // sel_rows
    allowed = (rank_k[None, :] <= rank_q[:, None])[None]
    scores = jnp.einsum("qhd,khd->hqk", query, piece_k, preferred_element_type=jnp.float32) * scale
    scores = jnp.where(allowed, scores, -1e30)
    newtop = jnp.maximum(top, jnp.max(scores, axis=-1))
    weights = jnp.where(allowed, jnp.exp(scores - newtop[..., None]), 0.0)
    total = jnp.sum(weights, axis=-1)
    summed = jnp.einsum(
        "hqk,khd->hqd", weights.astype(jnp.bfloat16), piece_v, preferred_element_type=jnp.float32
    )
    top, total, summed = (newtop, total, summed)
    attended = (
        jnp.transpose(summed / total[..., None], (1, 0, 2))
        .reshape(sel_rows, heads * HEAD_DIM)
        .astype(jnp.bfloat16)
    )
    update = jnp.dot(
        lax.all_gather(attended, "mp", axis=1, tiled=True),
        w_out,
        preferred_element_type=jnp.float32,
    )
    new_rows = (own_rows.astype(jnp.float32) + gate[:, None] * update).astype(jnp.bfloat16)
    backward = jnp.zeros((shards * bucket, part_width), jnp.bfloat16).at[fetch].set(new_rows)
    returned = lax.all_to_all(
        backward.reshape(shards, bucket, part_width), "seq", split_axis=0, concat_axis=0, tiled=True
    )
    taken = returned.reshape(shards * bucket, part_width)[jnp.where(live, cell, 0)]
    return jnp.where(live[:, None], taken, hidden)


def solution(mesh):
    placed = (
        P("seq", "mp"),
        P("seq"),
        P("seq"),
        P(),
        P(),
        P("seq", "mp"),
        P("seq", "mp"),
        P("seq", "mp"),
        P(None, "mp"),
    )
    return jax.shard_map(
        per_device, mesh=mesh, in_specs=placed, out_specs=P("seq", "mp"), check_vma=False
    )
```

profile of v0, /device:TPU:1, one launch (start us, length us, event | category | flops | bytes accessed | tf_op | source)
XLA Modules:
  0.0 546.8 jit_solution(13006435467055778807)
XLA Ops:
  6.5 0.7 fusion.44
  7.3 4.3 scatter_custom_fusion
  11.6 1.8 concatenate.11
  13.4 1.2 gather_fusion
  14.6 1.0 reshape.141
  15.6 13.2 %all-to-all-start = ((bf16[64,4,1024]{2,1,0:T(4,128)(2,1)}), bf16[64,4,1024]{2,1,0:T(4,128)(2,1)S(1)}, u32[]{:S(2)}, u32[]{:S(2)}) async-start(bf16[64,4,1024]{2,1,0:T(4,128)(2,1)} %reshape.141), calls=%async_computation | async-start | bytes 1048576 | tf_op jit(solution)/shard_map/all_to_all | solution.py:41
  28.7 0.0 all-gather.18.cloned.1.call-start
  28.8 17.6 %all-to-all-done = bf16[64,4,1024]{2,1,0:T(4,128)(2,1)S(1)} async-done(((bf16[64,4,1024]{2,1,0:T(4,128)(2,1)}), bf16[64,4,1024]{2,1,0:T(4,128)(2,1)S(1)}, u32[]{:S(2)}, u32[]{:S(2)}) %all-to-all-start) | async-done | bytes 524320 | tf_op jit(solution)/shard_map/all_to_all | solution.py:41
  46.4 0.1 reshape.142
  46.6 1.6 gather_fusion.1
  48.1 0.0 all-gather.10.cloned.1.call-start
  48.2 0.7 all-gather.10.cloned.1.call-update
  48.9 0.0 all-gather.8.cloned.1.call-start
  48.9 0.7 all-gather.8.cloned.1.call-update
  49.6 0.0 all-gather.14.cloned.1.call-start
  49.7 0.5 all-gather.14.cloned.1.call-update
  50.2 0.0 all-gather.12.cloned.1.call-start
  50.3 0.3 multiply_cosine_fusion
  50.6 19.6 %all-gather.18.cloned.1.call-done = bf16[128,4096]{1,0:T(8,128)(2,1)} async-done(((bf16[128,1024]{1,0:T(8,128)(2,1)}), bf16[128,4096]{1,0:T(8,128)(2,1)}) %all-gather.18.cloned.1.call-update) | async-done | bytes 1048592 | tf_op jit(solution)/shard_map/all_gather | solution.py:43
  70.3 1.6 fusion.6
  71.9 81.9 %all-gather.10.cloned.1.call-done = bf16[4096,512]{1,0:T(8,128)(2,1)} async-done(((bf16[64,512]{1,0:T(8,128)(2,1)}), bf16[4096,512]{1,0:T(8,128)(2,1)}) %all-gather.10.cloned.1.call-update) | async-done | bytes 4194320 | tf_op jit(solution)/shard_map/all_gather | solution.py:53
  153.8 3.3 fusion.55
  157.1 0.1 reshape.144
  157.2 75.7 %all-gather.8.cloned.1.call-done = bf16[4096,512]{1,0:T(8,128)(2,1)} async-done(((bf16[64,512]{1,0:T(8,128)(2,1)}), bf16[4096,512]{1,0:T(8,128)(2,1)}) %all-gather.8.cloned.1.call-update) | async-done | bytes 4194320 | tf_op jit(solution)/shard_map/all_gather | solution.py:52
  232.9 2.9 fusion.57
  235.8 0.1 reshape.143
  235.9 0.3 fusion.60
  236.3 0.1 subtract_convert_fusion.1
  236.4 0.8 pad_maximum_fusion
  237.2 0.2 all-gather.16.cloned.1.call-start
  237.5 74.4 %all-gather.14.cloned.1.call-done = bf16[4096,512]{1,0:T(8,128)(2,1)} async-done(((bf16[64,512]{1,0:T(8,128)(2,1)}), bf16[4096,512]{1,0:T(8,128)(2,1)}) %all-gather.14.cloned.1.call-update) | async-done | bytes 4194320 | tf_op jit(solution)/shard_map/all_gather | solution.py:54
  311.8 2.9 convolution_convert_fusion
  314.8 0.7 copy.15
  315.6 0.6 broadcast_compare_fusion
  316.3 0.4 fusion.17
  316.6 78.1 %all-gather.12.cloned.1.call-done = bf16[8192,4,128]{2,0,1:T(8,128)(2,1)} async-done(((bf16[128,4,128]{2,0,1:T(8,128)(2,1)}), bf16[8192,4,128]{2,0,1:T(8,128)(2,1)}) %all-gather.12.cloned.1.call-update) | async-done | bytes 8388624 | tf_op jit(solution)/shard_map/all_gather | solution.py:62
  394.8 12.7 %fusion = (f32[4,128]{1,0:T(4,128)S(1)}, f32[4,128,8192]{2,1,0:T(8,128)}) fusion(pred[128,8192]{1,0:T(8,128)(4,1)S(1)} %broadcast_compare_fusion, bf16[8192,4,128]{2,0,1:T(8,128)(2,1)} %all-gather.12.cloned.1.call-done, bf16[128,4,64]{2,0,1:T(8,128)(2,1)S(1)} %get-tuple-element.9, bf16[128,4,64]{2,0,1:T(8,128)(2,1)S(1)} %get-tuple-element.8), kind=kOutput, calls=%fused_computation.7 | convolution fusion | flops 1086586368 | bytes 26347520 | tf_op jit(solution)/shard_map/qhd,khd->hqk/dot_general | solution.py:67
  407.5 8.4 %fusion.1 = f32[4,128]{1,0:T(4,128)S(1)} fusion(f32[4,128,8192]{2,1,0:T(8,128)} %get-tuple-element.23, f32[4,128]{1,0:T(4,128)S(1)} %broadcast_maximum_fusion, pred[128,8192]{1,0:T(8,128)(4,1)S(1)} %broadcast_compare_fusion), kind=kLoop, calls=%fused_computation.8 | loop fusion | flops 20971008 | bytes 17829888 | tf_op jit(solution)/shard_map/reduce_sum | solution.py:71
  415.9 64.1 %all-gather.16.cloned.1.call-done = bf16[8192,4,128]{0,2,1:T(8,128)(2,1)} async-done(((bf16[128,4,128]{0,2,1:T(8,128)(2,1)}), bf16[8192,4,128]{0,2,1:T(8,128)(2,1)}) %all-gather.16.cloned.1.call-update) | async-done | bytes 8388624 | tf_op jit(solution)/shard_map/all_gather | solution.py:63
  480.0 10.7 %fusion.21 = bf16[128,4,128]{0,2,1:T(8,128)(2,1)S(1)} fusion(bf16[8192,4,128]{0,2,1:T(8,128)(2,1)} %all-gather.16.cloned.1.call-done, f32[4,128,8192]{2,1,0:T(8,128)} %get-tuple-element.23, f32[4,128]{1,0:T(4,128)S(1)} %broadcast_maximum_fusion, pred[128,8192]{1,0:T(8,128)(4,1)S(1)} %broadcast_compare_fusion, f32[128,4]{0,1:T(4,128)S(1)} %bitcast.30), kind=kOutput, calls=%fused_computation.30 | convolution fusion | flops 1094844416 | bytes 26349568 | tf_op jit(solution)/shard_map/hqk,khd->hqd/dot_general | solution.py:72
  490.7 11.0 %all_gather.27 = bf16[128,2048]{0,1:T(8,128)(2,1)S(1)} all-gather(bf16[128,512]{0,1:T(8,128)(2,1)S(1)} %bitcast.29), channel_id=1, replica_groups=mesh['seq'=64,'mp'=4] {'mp'}, dimensions={1}, use_global_device_ids=true | all-gather | bytes 655360 | tf_op jit(solution)/shard_map/all_gather | solution.py:82
  501.7 0.8 fusion.10
  502.5 1.3 scatter_custom_fusion.1
  503.8 0.2 reshape.145
  504.0 28.6 %all_to_all.10 = bf16[64,4,1024]{2,1,0:T(4,128)(2,1)S(1)} all-to-all(bf16[64,4,1024]{2,1,0:T(4,128)(2,1)S(1)} %reshape.145), channel_id=1, replica_groups=mesh['seq'=64,'mp'=4] {'seq'}, dimensions={0} | all-to-all | bytes 1048576 | tf_op jit(solution)/shard_map/all_to_all | solution.py:88
  532.6 0.1 reshape.146
  532.7 4.1 gather_fusion.2
  536.8 3.2 broadcast_select_fusion
  (28 shorter events, 0.2 us)
Async XLA Ops:
  13.4 15.4 %copy-start.5 = (s32[128]{0:T(128)S(1)}, s32[128]{0:T(128)}, u32[]{:S(2)}) copy-start(s32[128]{0:T(128)} %param.10) | copy-start | bytes 1540
  13.4 36.9 %copy-start.3 = (bf16[4096]{0:T(1024)(128)(2,1)S(1)}, bf16[4096]{0:T(1024)(128)(2,1)}, u32[]{:S(2)}) copy-start(bf16[4096]{0:T(1024)(128)(2,1)} %param.12) | copy-start | bytes 24580
  15.6 30.9 %all-to-all-start = ((bf16[64,4,1024]{2,1,0:T(4,128)(2,1)}), bf16[64,4,1024]{2,1,0:T(4,128)(2,1)S(1)}, u32[]{:S(2)}, u32[]{:S(2)}) async-start(bf16[64,4,1024]{2,1,0:T(4,128)(2,1)} %reshape.141), calls=%async_computation | async-start | bytes 1048576 | tf_op jit(solution)/shard_map/all_to_all | solution.py:41
  28.7 41.5 %all-gather.18.cloned.1.call-start = ((), (), s32[]{:S(2)}) async-start(), calls=%async_computation.7 | async-start | bytes 1310720 | tf_op jit(solution)/shard_map/all_gather | solution.py:43
  48.1 105.6 %all-gather.10.cloned.1.call-start = ((), (), s32[]{:S(2)}) async-start(), calls=%async_computation.3 | async-start | bytes 4259840 | tf_op jit(solution)/shard_map/all_gather | solution.py:53
  48.9 184.0 %all-gather.8.cloned.1.call-start = ((), (), s32[]{:S(2)}) async-start(), calls=%async_computation.2 | async-start | bytes 4259840 | tf_op jit(solution)/shard_map/all_gather | solution.py:52
  49.6 262.2 %all-gather.14.cloned.1.call-start = ((), (), s32[]{:S(2)}) async-start(), calls=%async_computation.5 | async-start | bytes 4259840 | tf_op jit(solution)/shard_map/all_gather | solution.py:54
  50.2 344.6 %all-gather.12.cloned.1.call-start = ((), (), s32[]{:S(2)}) async-start(), calls=%async_computation.4 | async-start | bytes 8519680 | tf_op jit(solution)/shard_map/all_gather | solution.py:62
  70.3 162.6 %copy-start.1 = (bf16[128,4096]{1,0:T(8,128)(2,1)S(1)}, bf16[128,4096]{1,0:T(8,128)(2,1)}, u32[]{:S(2)}) copy-start(bf16[128,4096]{1,0:T(8,128)(2,1)} %all-gather.18.cloned.1.call-done) | copy-start | bytes 3145732
  236.3 79.3 %copy-start.4 = (bf16[4096]{0:T(1024)(128)(2,1)S(1)}, bf16[4096]{0:T(1024)(128)(2,1)}, u32[]{:S(2)}) copy-start(bf16[4096]{0:T(1024)(128)(2,1)} %param.13) | copy-start | bytes 24580
  237.2 242.8 %all-gather.16.cloned.1.call-start = ((), (), s32[]{:S(2)}) async-start(), calls=%async_computation.6 | async-start | bytes 8519680 | tf_op jit(solution)/shard_map/all_gather | solution.py:63
  480.0 21.7 %copy-start = (bf16[2048,1024]{1,0:T(8,128)(2,1)S(1)}, bf16[2048,1024]{1,0:T(8,128)(2,1)}, u32[]{:S(2)}) copy-start(bf16[2048,1024]{1,0:T(8,128)(2,1)} %param.17) | copy-start | bytes 12582916
  480.0 21.7 %copy-start.2 = (bf16[128,1024]{1,0:T(8,128)(2,1)S(1)}, bf16[128,1024]{1,0:T(8,128)(2,1)}, u32[]{:S(2)}) copy-start(bf16[128,1024]{1,0:T(8,128)(2,1)} %gather_fusion.1) | copy-start | bytes 786436
Sparse Core Ops, SparseCore 0:
  48.3 21.9 all-gather.17
  73.0 80.7 all-gather.9
  156.6 76.2 all-gather.7
  235.5 76.2 all-gather.13
  314.5 80.2 all-gather.11
  397.3 82.6 all-gather.15
where the time goes:
time: 547 us
  waiting for transfers between devices  413 us (76%)
  blocking collectives  39.5 us (7%)
  matrix products  33.7 us (6%)
  local copies, waits for them, and re-layouts  16.9 us (3%)
  other arithmetic  15.8 us (3%)
  between operations  13.7 us (3%)
  starting transfers between devices  13.6 us (2%)
    all_gather x1, waiting for transfers between devices, per_device(): key_raw = add_rows(lax.all_gather(w_key, 'seq', axis=0, tiled=True))  81.9 us
    all_gather x1, waiting for transfers between devices, per_device(): piece_k = lax.all_gather(keys, 'seq', axis=0, tiled=True)  78.1 us
    all_gather x1, waiting for transfers between devices, per_device(): query_raw = add_rows(lax.all_gather(w_query, 'seq', axis=0, tiled=True))  75.7 us
    all_gather x1, waiting for transfers between devices, per_device(): value_raw = add_rows(lax.all_gather(w_value, 'seq', axis=0, tiled=True))  74.4 us
    all_gather x1, waiting for transfers between devices, per_device(): piece_v = lax.all_gather(values, 'seq', axis=0, tiled=True)  64.1 us
    all_to_all x1, blocking collectives, per_device(): lax.all_to_all(backward.reshape(shards, bucket, part_width), 'seq', split...  28.6 us
    all_gather x1, waiting for transfers between devices, per_device(): full_rows = lax.all_gather(own_rows, 'mp', axis=1, tiled=True)  19.6 us
    all_to_all x1, waiting for transfers between devices, per_device(): lax.all_to_all(outgoing, 'seq', split_axis=0, concat_axis=0, tiled=True)  17.6 us
  transfers between devices with their start and end apart: 7, of which 7 were waited for; matrix products, arithmetic and copies ran while one was open for 6% of the time, Pallas kernels for 0%

commit v1 on v0

v1 whole, which is shorter than its diff:
```python
import functools
import math

import jax
import jax.numpy as jnp
from jax import lax
from jax.experimental import pallas as pl
from jax.experimental.pallas import tpu as pltpu
from jax.sharding import Mesh, PartitionSpec as P

HEAD_DIM = 128
SEL_DEV = 128
NZ, NY, NC, NX = 8, 4, 2, 4
SHARDS = NZ * NY * NC
BUCKET = 4
BF16, F32, I32 = jnp.bfloat16, jnp.float32, jnp.int32
QSCALE = math.log2(math.e) / math.sqrt(HEAD_DIM)
NEG = -1e30


def project_kernel(rows_ref, w_ref, cos_ref, sin_ref, q_ref, kv_ref):
    acc = jnp.zeros((SEL_DEV, 3 * HEAD_DIM), F32)
    squares = jnp.zeros((SEL_DEV, 1), F32)
    for x in range(NX):
        piece = rows_ref[0, x]
        acc += jnp.dot(piece, w_ref[x * 1024 : (x + 1) * 1024, :], preferred_element_type=F32)
        wide = piece.astype(F32)
        squares += jnp.sum(wide * wide, axis=-1, keepdims=True)
    acc = acc * lax.rsqrt(squares * (1.0 / 4096) + 1e-05)
    cosine, sine = cos_ref[0], sin_ref[0]

    def turn(a):
        return a * cosine + pltpu.roll(a, 64, 1) * sine

    q_ref[0] = (turn(acc[:, :128]) * QSCALE).astype(BF16)
    kv_ref[0] = jnp.concatenate([turn(acc[:, 128:256]), acc[:, 256:]], axis=-1).astype(BF16)


def project(rows, w, cosine, sine):
    tile = lambda *tail: pl.BlockSpec((1,) + tail, lambda i: (i,) + (0,) * len(tail))
    return pl.pallas_call(
        project_kernel,
        grid=(NY,),
        in_specs=[
            tile(NX, SEL_DEV, 1024),
            pl.BlockSpec((4096, 384), lambda i: (0, 0)),
            tile(SEL_DEV, 128),
            tile(SEL_DEV, 128),
        ],
        out_specs=[tile(SEL_DEV, 128), tile(SEL_DEV, 256)],
        out_shape=[
            jax.ShapeDtypeStruct((NY, SEL_DEV, 128), BF16),
            jax.ShapeDtypeStruct((NY, SEL_DEV, 256), BF16),
        ],
        compiler_params=pltpu.CompilerParams(vmem_limit_bytes=32 << 20),
    )(rows, w, cosine, sine)


def attend_kernel(off_ref, q_ref, kv_ref, o_ref, qs, top, total, acc):
    for b in range(4):
        for y in range(NY):
            qs[b * 128 + y * 32 : b * 128 + y * 32 + 32] = q_ref[y, b * 32 : b * 32 + 32]
    top[...] = jnp.full(top.shape, NEG, F32)
    total[...] = jnp.zeros(total.shape, F32)
    acc[...] = jnp.zeros(acc.shape, F32)
    row = lax.broadcasted_iota(I32, (128, 512), 0)
    col = lax.broadcasted_iota(I32, (128, 512), 1)
    rank_q = row % 32 * 64 + row // 32 * 2 + off_ref[0]
    for b in range(4):
        live = slice(b * 128, 512)
        for part in range(4):
            block = kv_ref[part * 4 : part * 4 + 4, :, b * 32 : b * 32 + 32, :].reshape(512, 256)
            scores = lax.dot_general(
                qs[live], block[:, :128], (((1,), (1,)), ((), ())), preferred_element_type=F32
            )
            group = part * 4 + col // 128
            rank_k = col % 32 * 64 + col // 32 % 4 * 2 + group // 2 * 8 + group % 2
            edge = jnp.where(rank_k <= rank_q, scores[:128], NEG)
            scores = edge if b == 3 else jnp.concatenate([edge, scores[128:]], axis=0)
            old = top[live, :1]
            new = jnp.maximum(old, jnp.max(scores, axis=-1, keepdims=True))
            weights = jnp.exp2(scores - new)
            shrink = jnp.exp2(old - new)
            top[live] = jnp.broadcast_to(new, (512 - b * 128, 128))
            total[live] = total[live] * shrink + jnp.sum(weights, axis=-1, keepdims=True)
            acc[live] = acc[live] * shrink + jnp.dot(
                weights.astype(BF16), block[:, 128:], preferred_element_type=F32
            )
    done = (acc[...] / total[...]).astype(BF16)
    for b in range(4):
        for y in range(NY):
            o_ref[y, b * 32 : b * 32 + 32] = done[b * 128 + y * 32 : b * 128 + y * 32 + 32]


def attend(offset, query, keys_values):
    whole = pl.BlockSpec(memory_space=pltpu.VMEM)
    return pl.pallas_call(
        attend_kernel,
        in_specs=[pl.BlockSpec(memory_space=pltpu.SMEM), whole, whole],
        out_specs=whole,
        out_shape=jax.ShapeDtypeStruct((NY, SEL_DEV, 128), BF16),
        scratch_shapes=[
            pltpu.VMEM((512, 128), BF16),
            pltpu.VMEM((512, 128), F32),
            pltpu.VMEM((512, 128), F32),
            pltpu.VMEM((512, 128), F32),
        ],
        compiler_params=pltpu.CompilerParams(vmem_limit_bytes=32 << 20),
    )(offset, query, keys_values)


def around(array, axis, size):
    here = lax.axis_index(axis)
    got = [array] + [
        lax.ppermute(array, axis, [(i, (i + k) % size) for i in range(size)]) for k in range(1, size)
    ]
    stacked = jnp.stack(got)
    return stacked[(here - jnp.arange(size)) % size]


def per_device(hidden, picked, target, norm_gain, router_weight, w_query, w_key, w_value, w_out):
    z, y, c = lax.axis_index("z"), lax.axis_index("y"), lax.axis_index("c")
    shard = (z * NY + y) * NC + c

    gain = lax.dynamic_slice(norm_gain, (shard * 64,), (64,)).astype(F32)
    mine = jnp.concatenate(
        [w.reshape(64, NY, HEAD_DIM) for w in (w_query, w_key, w_value)], axis=-1
    ).transpose(1, 0, 2)
    mine = (mine.astype(F32) * gain[None, :, None]).astype(BF16)
    heads = lax.all_to_all(mine, "y", split_axis=0, concat_axis=0, tiled=True)
    weights = lax.all_gather(heads, ("z", "c"), axis=0, tiled=True)
    weights = weights.reshape(NZ, NC, NY, 64, 384).transpose(0, 2, 1, 3, 4).reshape(4096, 384)

    places = around(picked, "y", NY)
    half = HEAD_DIM // 2
    freq = jnp.exp(-math.log(10000.0) * (2.0 * jnp.arange(half, dtype=F32) / HEAD_DIM))
    angle = places.astype(F32)[..., None] * freq
    cosine, sine = jnp.cos(angle), jnp.sin(angle)
    cosine = jnp.concatenate([cosine, cosine], axis=-1)
    sine = jnp.concatenate([-sine, sine], axis=-1)

    live = target >= 0
    cell = jnp.where(live, target // SEL_DEV * BUCKET + target % BUCKET, -1)
    slots = jnp.arange(SHARDS * BUCKET, dtype=I32)
    pick_out = (cell[None, :] == slots[:, None]).astype(BF16)
    outgoing = jnp.dot(pick_out, hidden, preferred_element_type=F32).astype(BF16)
    arrived = lax.all_to_all(
        outgoing.reshape(SHARDS, BUCKET, -1), ("z", "y", "c"), split_axis=0, concat_axis=0, tiled=True
    ).reshape(SHARDS * BUCKET, -1)
    fetch = picked // hidden.shape[0] * BUCKET + jnp.arange(SEL_DEV, dtype=I32) % BUCKET
    pick_in = (fetch[:, None] == slots[None, :]).astype(BF16)
    own_rows = jnp.dot(pick_in, arrived, preferred_element_type=F32).astype(BF16)

    rows = lax.all_gather(own_rows, ("y", "x"), axis=0).reshape(NY, NX, SEL_DEV, 1024)
    query, mine_kv = project(rows, weights, cosine, sine)
    full = lax.dynamic_index_in_dim(rows, y, 0, keepdims=False)
    gate = jax.nn.sigmoid(
        jnp.einsum("xrf,xf->r", full, router_weight.reshape(NX, 1024), preferred_element_type=F32)
    )
    keys_values = lax.all_gather(mine_kv, ("z", "c"), axis=0)
    offset = (z * 8 + c).astype(I32).reshape(1)
    attended = attend(offset, query, keys_values)

    by_head = lax.all_to_all(attended, "y", split_axis=0, concat_axis=0, tiled=True)
    all_heads = lax.all_gather(by_head, "x", axis=0, tiled=True)
    flat = all_heads.transpose(1, 0, 2).reshape(SEL_DEV, 16 * HEAD_DIM)
    update = jnp.dot(flat, w_out, preferred_element_type=F32)
    new_rows = (own_rows.astype(F32) + gate[:, None] * update).astype(BF16)
    backward = jnp.dot(pick_in.T, new_rows, preferred_element_type=F32).astype(BF16)
    returned = lax.all_to_all(
        backward.reshape(SHARDS, BUCKET, -1), ("z", "y", "c"), split_axis=0, concat_axis=0, tiled=True
    ).reshape(SHARDS * BUCKET, -1)
    taken = jnp.dot(pick_out.T, returned, preferred_element_type=F32).astype(BF16)
    return jnp.where(live[:, None], taken, hidden)


def solution(mesh):
    cut = Mesh(mesh.devices.reshape(NZ, NY, NC, NX), ("z", "y", "c", "x"))
    seq = ("z", "y", "c")
    placed = (
        P(seq, "x"),
        P(seq),
        P(seq),
        P(),
        P(),
        P(seq, "x"),
        P(seq, "x"),
        P(seq, "x"),
        P(None, "x"),
    )
    return jax.shard_map(
        per_device, mesh=cut, in_specs=placed, out_specs=P(seq, "x"), check_vma=False
    )
```

time: 547 us -> 251 us (0.46)
  waiting for transfers between devices: 413 us -> 146 us
  matrix products: 33.7 us -> 10.4 us
  blocking collectives: 39.5 us -> 20.8 us
  starting transfers between devices: 13.6 us -> 29.3 us
  Pallas kernels: 0 us -> 12.7 us
  other arithmetic: 15.8 us -> 3.54 us
    all_gather x6 -> x3, waiting for transfers between devices: 394 us -> 98.9 us  [the longest x1 55.4 us: per_device(): lax.all_gather(own_rows, ('y', 'x'), axis=0).reshape(NY, NX, SEL_DEV, 1024)]
    all_to_all x1 -> x3, waiting for transfers between devices: 17.6 us -> 44.1 us  [the longest x1 23.2 us: per_device(): lax.all_to_all(outgoing.reshape(SHARDS, BUCKET, -1), ('z', 'y', 'c'), spl...]
    dot_general x7 -> x5, matrix products: 33.7 us -> 10.4 us  [the longest x1 3.32 us: per_device(): jnp.dot(pick_in.T, new_rows, preferred_element_type=F32).astype(BF16)]
    all_to_all x1, blocking collectives: 28.6 us -> 10.1 us  [per_device(): heads = lax.all_to_all(mine, 'y', split_axis=0, concat_axis=0, tiled=True)]
    pallas_call x0 -> x2, Pallas kernels: none -> 12.7 us  [the longest x1 9.52 us: attend(): pl.pallas_call(attend_kernel, in_specs=[pl.BlockSpec(memory_space=pltpu.S...]
    all_to_all x1 -> x3, starting transfers between devices: 13.2 us -> 25.7 us  [the longest x1 11.7 us: per_device(): lax.all_to_all(outgoing.reshape(SHARDS, BUCKET, -1), ('z', 'y', 'c'), spl...]
    reduce_sum x2 -> x0, other arithmetic: 9.98 us -> none  [the longest x1 8.38 us: per_device(): total = jnp.sum(weights, axis=-1)]
    gather x3 -> x1, local copies, waits for them, and re-layouts: 6.8 us -> 0.56 us  [around(): return stacked[(here - jnp.arange(size)) % size]]
  transfers between devices with their start and end apart: 7 -> 9, of which waited for: 7 -> 8; matrix products, arithmetic and copies ran while one was open for 6% -> 5% of each run, Pallas kernels for 0% -> 0%
where the time goes in v1:
time: 251 us; the launch traced here: 250 us
  waiting for transfers between devices  146 us (58%)
  starting transfers between devices  29.3 us (12%)
  blocking collectives  20.8 us (8%)
  local copies, waits for them, and re-layouts  14.1 us (6%)
  between operations  13.3 us (5%)
  Pallas kernels  12.7 us (5%)
  matrix products  10.4 us (4%)
  other arithmetic  3.54 us (1%)
    all_gather x1, waiting for transfers between devices, per_device(): lax.all_gather(own_rows, ('y', 'x'), axis=0).reshape(NY, NX, SEL_DEV, 1024)  55.4 us
    all_gather x1, waiting for transfers between devices, per_device(): keys_values = lax.all_gather(mine_kv, ('z', 'c'), axis=0)  42.4 us
    all_to_all x1, waiting for transfers between devices, per_device(): lax.all_to_all(outgoing.reshape(SHARDS, BUCKET, -1), ('z', 'y', 'c'), spl...  23.2 us
    all_to_all x1, waiting for transfers between devices, per_device(): lax.all_to_all(backward.reshape(SHARDS, BUCKET, -1), ('z', 'y', 'c'), spl...  17.7 us
    all_to_all x1, starting transfers between devices, per_device(): lax.all_to_all(outgoing.reshape(SHARDS, BUCKET, -1), ('z', 'y', 'c'), spl...  11.7 us
    all_gather x1, blocking collectives, per_device(): all_heads = lax.all_gather(by_head, 'x', axis=0, tiled=True)  10.7 us
    all_to_all x1, blocking collectives, per_device(): heads = lax.all_to_all(mine, 'y', split_axis=0, concat_axis=0, tiled=True)  10.1 us
    all_to_all x1, starting transfers between devices, per_device(): lax.all_to_all(backward.reshape(SHARDS, BUCKET, -1), ('z', 'y', 'c'), spl...  9.99 us
  transfers between devices with their start and end apart: 9, of which 8 were waited for; matrix products, arithmetic and copies ran while one was open for 5% of the time, Pallas kernels for 0%

profile of v1, /device:TPU:1, one launch (start us, length us, event | category | flops | bytes accessed | tf_op | source)
XLA Modules:
  0.0 250.3 jit_solution(15353763006592815041)
XLA Ops:
  6.5 0.9 reshape.106
  7.4 0.9 reshape.107
  8.3 0.9 reshape.108
  9.1 0.8 dynamic-slice_convert_fusion
  9.9 0.1 fusion.12
  10.1 10.1 %all_to_all.20 = bf16[4,64,384]{2,1,0:T(8,128)(2,1)} all-to-all(bf16[4,64,384]{2,1,0:T(8,128)(2,1)S(1)} %copy.15), channel_id=1, replica_groups=mesh['z'=8,'y'=4,'c'=2,'x'=4] {'y'}, dimensions={0} | all-to-all | bytes 393216 | tf_op jit(solution)/shard_map/all_to_all | solution.py:130
  20.2 0.0 all-gather.6.cloned.1.call-update
  20.2 0.7 fusion.19
  20.9 2.3 convolution_convert_fusion
  23.2 1.0 reshape.101
  24.2 11.7 %all-to-all-start = ((bf16[64,4,1024]{2,1,0:T(4,128)(2,1)}), bf16[64,4,1024]{2,1,0:T(4,128)(2,1)S(1)}, u32[]{:S(2)}, u32[]{:S(2)}) async-start(bf16[64,4,1024]{2,1,0:T(4,128)(2,1)} %reshape.101), calls=%async_computation | async-start | bytes 1048576 | tf_op jit(solution)/shard_map/all_to_all | solution.py:147
  35.9 0.0 all-gather.8.cloned.1.call-start
  36.0 23.2 %all-to-all-done = bf16[64,4,1024]{2,1,0:T(4,128)(2,1)S(1)} async-done(((bf16[64,4,1024]{2,1,0:T(4,128)(2,1)}), bf16[64,4,1024]{2,1,0:T(4,128)(2,1)S(1)}, u32[]{:S(2)}, u32[]{:S(2)}) %all-to-all-start) | async-done | bytes 524320 | tf_op jit(solution)/shard_map/all_to_all | solution.py:147
  59.2 0.1 reshape.102
  59.3 1.0 convolution_convert_fusion.2
  60.3 0.0 all-gather.8.cloned.1.call-update
  60.3 0.0 all-gather.10.cloned.1.call-start
  60.4 1.1 collective-permute-start
  61.4 1.7 collective-permute-start.2
  63.1 0.7 collective-permute-start.1
  63.9 0.6 collective-permute-done
  64.4 2.6 %collective-permute-done.1 = s32[128]{0:T(128)S(1)} collective-permute-done((s32[128]{0:T(128)S(1)}, s32[128]{0:T(128)S(1)}, u32[]{:S(2)}, u32[]{:S(2)}) %collective-permute-start.1) | collective-permute-done | bytes 544 | tf_op jit(solution)/shard_map/ppermute | solution.py:115
  67.0 0.6 gather_fusion
  67.6 1.0 fusion.13
  68.6 0.9 pad_maximum_fusion
  69.5 1.1 all-gather.6.cloned.1.call-done
  70.6 2.3 copy.16
  73.0 55.4 %all-gather.8.cloned.1.call-done = bf16[2048,1024]{1,0:T(8,128)(2,1)} async-done(((bf16[128,1024]{1,0:T(8,128)(2,1)}), bf16[2048,1024]{1,0:T(8,128)(2,1)}) %all-gather.8.cloned.1.call-update) | async-done | bytes 4194320 | tf_op jit(solution)/shard_map/all_gather | solution.py:154
  128.3 2.2 copy-done
  130.5 0.9 copy-done.2
  131.5 3.2 %shard_map.91 = (bf16[4,128,128]{2,1,0:T(8,128)(2,1)S(1)}, bf16[4,128,256]{2,1,0:T(8,128)(2,1)S(1)}) custom-call(bf16[4,4,128,1024]{3,2,1,0:T(8,128)(2,1)S(1)} %bitcast.39, bf16[4096,384]{1,0:T(8,128)(2,1)S(1)} %bitcast.37, f32[4,128,128]{2,1,0:T(8,128)S(1)} %get-tuple-element.12.cos_ref, f32[4,128,128]{2,1,0:T(8,128)S(1)} %copy-done.2), custom_call_target="tpu_custom_call" | custom-call | tf_op jit(solution)/shard_map/pallas_call | solution.py:41
  134.7 0.7 copy-done.3
  135.4 0.0 all-gather.10.cloned.1.call-update
  135.5 42.4 %all-gather.10.cloned.1.call-done = bf16[64,128,256]{2,1,0:T(8,128)(2,1)} async-done(((bf16[4,128,256]{2,1,0:T(8,128)(2,1)}), bf16[64,128,256]{2,1,0:T(8,128)(2,1)}) %all-gather.10.cloned.1.call-update) | async-done | bytes 4194320 | tf_op jit(solution)/shard_map/all_gather | solution.py:160
  177.8 2.2 copy-done.1
  180.0 9.5 %shard_map.92 = bf16[4,128,128]{2,1,0:T(8,128)(2,1)} custom-call(s32[1]{0:T(128)} %bitcast.3.off_ref, bf16[4,128,128]{2,1,0:T(8,128)(2,1)S(1)} %get-tuple-element.7.q_ref, bf16[16,4,128,256]{3,2,1,0:T(8,128)(2,1)S(1)} %bitcast.40), custom_call_target="tpu_custom_call" | custom-call | tf_op jit(solution)/shard_map/pallas_call | solution.py:97
  189.6 4.0 %all-to-all-start.2 = ((bf16[4,128,128]{2,1,0:T(8,128)(2,1)}), bf16[4,128,128]{2,1,0:T(8,128)(2,1)S(1)}, u32[]{:S(2)}, u32[]{:S(2)}) async-start(bf16[4,128,128]{2,1,0:T(8,128)(2,1)} %shard_map.92), calls=%async_computation.2 | async-start | bytes 262144 | tf_op jit(solution)/shard_map/all_to_all | solution.py:164
  193.6 1.6 fusion.5
  195.2 3.2 %all-to-all-done.2 = bf16[4,128,128]{2,1,0:T(8,128)(2,1)S(1)} async-done(((bf16[4,128,128]{2,1,0:T(8,128)(2,1)}), bf16[4,128,128]{2,1,0:T(8,128)(2,1)S(1)}, u32[]{:S(2)}, u32[]{:S(2)}) %all-to-all-start.2) | async-done | bytes 131104 | tf_op jit(solution)/shard_map/all_to_all | solution.py:164
  198.4 10.7 %all_gather.23 = bf16[16,128,128]{2,1,0:T(8,128)(2,1)S(1)} all-gather(bf16[4,128,128]{2,1,0:T(8,128)(2,1)S(1)} %all-to-all-done.2), channel_id=1, replica_groups=mesh['z'=8,'y'=4,'c'=2,'x'=4] {'x'}, dimensions={0}, use_global_device_ids=true | all-gather | bytes 655360 | tf_op jit(solution)/shard_map/all_gather | solution.py:165
  209.1 0.3 copy.17
  209.4 0.0 copy-start.8
  209.4 3.3 %convolution_convert_fusion.1 = bf16[256,1024]{1,0:T(8,128)(2,1)S(1)} fusion(bf16[128,2048]{0,1:T(8,128)(2,1)S(1)} %bitcast.42, bf16[2048,1024]{1,0:T(8,128)(2,1)} %param.17, bf16[128,1024]{1,0:T(8,128)(2,1)S(1)} %copy-done.4, f32[128]{0:T(128)S(1)} %fusion.5, s32[128]{0:T(128)S(1)} %fusion.22), kind=kOutput, calls=%fused_computation.3 | convolution fusion | flops 604798976 | bytes 5506048 | tf_op jit(solution)/shard_map/dot_general | solution.py:169
  212.7 1.0 reshape.112
  213.7 10.0 %all-to-all-start.3 = ((bf16[64,4,1024]{2,1,0:T(4,128)(2,1)}), bf16[64,4,1024]{2,1,0:T(4,128)(2,1)S(1)}, u32[]{:S(2)}, u32[]{:S(2)}) async-start(bf16[64,4,1024]{2,1,0:T(4,128)(2,1)} %reshape.112), calls=%async_computation.3 | async-start | bytes 1048576 | tf_op jit(solution)/shard_map/all_to_all | solution.py:170
  223.7 17.7 %all-to-all-done.3 = bf16[64,4,1024]{2,1,0:T(4,128)(2,1)S(1)} async-done(((bf16[64,4,1024]{2,1,0:T(4,128)(2,1)}), bf16[64,4,1024]{2,1,0:T(4,128)(2,1)S(1)}, u32[]{:S(2)}, u32[]{:S(2)}) %all-to-all-start.3) | async-done | bytes 524320 | tf_op jit(solution)/shard_map/all_to_all | solution.py:170
  241.4 0.1 reshape.113
  241.6 2.2 convert_select_fusion
  (24 shorter events, 0.1 us)
Async XLA Ops:
  6.5 29.4 %copy-start.7 = (s32[128]{0:T(128)S(1)}, s32[128]{0:T(128)}, u32[]{:S(2)}) copy-start(s32[128]{0:T(128)} %param.10) | copy-start | bytes 1540
  6.5 64.1 %all-gather.6.cloned.1.call-start = ((), (), s32[]{:S(2)}) async-start(), calls=%async_computation.4 | async-start | bytes 3342336 | tf_op jit(solution)/shard_map/all_gather | solution.py:131
  24.2 35.0 %all-to-all-start = ((bf16[64,4,1024]{2,1,0:T(4,128)(2,1)}), bf16[64,4,1024]{2,1,0:T(4,128)(2,1)S(1)}, u32[]{:S(2)}, u32[]{:S(2)}) async-start(bf16[64,4,1024]{2,1,0:T(4,128)(2,1)} %reshape.101), calls=%async_computation | async-start | bytes 1048576 | tf_op jit(solution)/shard_map/all_to_all | solution.py:147
  35.9 92.4 %all-gather.8.cloned.1.call-start = ((), (), s32[]{:S(2)}) async-start(), calls=%async_computation.5 | async-start | bytes 4456448 | tf_op jit(solution)/shard_map/all_gather | solution.py:154
  60.3 117.5 %all-gather.10.cloned.1.call-start = ((), (), s32[]{:S(2)}) async-start(), calls=%async_computation.6 | async-start | bytes 4456448 | tf_op jit(solution)/shard_map/all_gather | solution.py:160
  60.4 4.1 %collective-permute-start = (s32[128]{0:T(128)S(1)}, s32[128]{0:T(128)S(1)}, u32[]{:S(2)}, u32[]{:S(2)}) collective-permute-start(s32[128]{0:T(128)S(1)} %copy-done.7), channel_id=1, source_target_pairs={{0,8},{8,16},{16,24},{24,0},{1,9},{9,17},{17,25},{25,1},{2,10},{10... | collective-permute-start | bytes 1544 | tf_op jit(solution)/shard_map/ppermute | solution.py:115
  61.4 3.0 %collective-permute-start.2 = (s32[128]{0:T(128)S(1)}, s32[128]{0:T(128)S(1)}, u32[]{:S(2)}, u32[]{:S(2)}) collective-permute-start(s32[128]{0:T(128)S(1)} %copy-done.7), channel_id=1, source_target_pairs={{0,24},{8,0},{16,8},{24,16},{1,25},{9,1},{17,9},{25,17},{2,26},{10... | collective-permute-start | bytes 1544 | tf_op jit(solution)/shard_map/ppermute | solution.py:115
  63.1 3.9 %collective-permute-start.1 = (s32[128]{0:T(128)S(1)}, s32[128]{0:T(128)S(1)}, u32[]{:S(2)}, u32[]{:S(2)}) collective-permute-start(s32[128]{0:T(128)S(1)} %copy-done.7), channel_id=1, source_target_pairs={{0,16},{8,24},{16,0},{24,8},{1,17},{9,25},{17,1},{25,9},{2,18},{10... | collective-permute-start | bytes 1544 | tf_op jit(solution)/shard_map/ppermute | solution.py:115
  70.6 64.8 %copy-start.6 = (bf16[4096]{0:T(1024)(128)(2,1)S(1)}, bf16[4096]{0:T(1024)(128)(2,1)}, u32[]{:S(2)}) copy-start(bf16[4096]{0:T(1024)(128)(2,1)} %param.13) | copy-start | bytes 24580
  128.3 2.2 copy-start
  130.5 0.9 copy-start.2
  134.7 0.7 copy-start.3
  135.4 74.0 %copy-start.4 = (bf16[128,1024]{1,0:T(8,128)(2,1)S(1)}, bf16[128,1024]{1,0:T(8,128)(2,1)}, u32[]{:S(2)}) copy-start(bf16[128,1024]{1,0:T(8,128)(2,1)} %convolution_convert_fusion.2) | copy-start | bytes 786436
  177.8 2.2 copy-start.1
  189.6 8.8 %all-to-all-start.2 = ((bf16[4,128,128]{2,1,0:T(8,128)(2,1)}), bf16[4,128,128]{2,1,0:T(8,128)(2,1)S(1)}, u32[]{:S(2)}, u32[]{:S(2)}) async-start(bf16[4,128,128]{2,1,0:T(8,128)(2,1)} %shard_map.92), calls=%async_computation.2 | async-start | bytes 262144 | tf_op jit(solution)/shard_map/all_to_all | solution.py:164
  209.1 14.6 %copy-start.5 = (s32[1024]{0:T(1024)S(1)}, s32[1024]{0:T(1024)}, u32[]{:S(2)}) copy-start(s32[1024]{0:T(1024)} %param.11) | copy-start | bytes 12292
  209.4 32.2 %copy-start.8 = (bf16[1024,1024]{1,0:T(8,128)(2,1)S(1)}, bf16[1024,1024]{1,0:T(8,128)(2,1)}, u32[]{:S(2)}) copy-start(bf16[1024,1024]{1,0:T(8,128)(2,1)} %param.9) | copy-start | bytes 6291460
  213.7 27.7 %all-to-all-start.3 = ((bf16[64,4,1024]{2,1,0:T(4,128)(2,1)}), bf16[64,4,1024]{2,1,0:T(4,128)(2,1)S(1)}, u32[]{:S(2)}, u32[]{:S(2)}) async-start(bf16[64,4,1024]{2,1,0:T(4,128)(2,1)} %reshape.112), calls=%async_computation.3 | async-start | bytes 1048576 | tf_op jit(solution)/shard_map/all_to_all | solution.py:170
Sparse Core Ops, SparseCore 0:
  20.3 50.2 all-gather.5
  73.0 55.2 all-gather.7
  135.5 42.2 all-gather.9

commit v2 on v1

v2 whole, which is shorter than its diff:
```python
import functools
import math

import jax
import jax.numpy as jnp
from jax import lax
from jax.experimental import pallas as pl
from jax.experimental.pallas import tpu as pltpu
from jax.sharding import Mesh, PartitionSpec as P

HEAD_DIM = 128
SEL_DEV = 128
NZ, NY, NC, NX = 8, 4, 2, 4
SHARDS = NZ * NY * NC
BUCKET = 4
BF16, F32, I32 = jnp.bfloat16, jnp.float32, jnp.int32
QSCALE = math.log2(math.e) / math.sqrt(HEAD_DIM)
NEG = -1e30


def shift(array, axis, by, size):
    return lax.ppermute(array, axis, [(i, (i + by) % size) for i in range(size)])


def project_kernel(where_ref, over_x, over_y, far_a, far_b, w_ref, cos_ref, sin_ref, out_ref):
    z, y, c, x = (where_ref[i] for i in range(4))

    def rows(half, i):
        span = slice(half * 64, half * 64 + 64)
        got = [over_x[(x + i) & 3, span]]
        for r in range(1, NY):
            if i == 0:
                got.append(over_y[(y + r) & 3, span])
            elif half == 0:
                got.append(far_a[(y + r) & 3, i - 1])
            else:
                got.append(far_b[(x + i) & 3, r - 1])
        return jnp.concatenate(got, axis=0)

    def turn(a, cosine, sine):
        return a * cosine + pltpu.roll(a, 64, 1) * sine

    for half in range(2):
        span = slice(half * 64, half * 64 + 64)
        acc = jnp.zeros((256, 3 * HEAD_DIM), F32)
        squares = jnp.zeros((256, 128), F32)
        for i in range(NX):
            piece = rows(half, i)
            for j in range(2):
                away = ((((x + i) & 3) * 2 + j - z) * (1 - 2 * c)) & 7
                acc += jnp.dot(
                    piece[:, j * 512 : j * 512 + 512], w_ref[away], preferred_element_type=F32
                )
            for j in range(8):
                wide = piece[:, j * 128 : j * 128 + 128].astype(F32)
                squares += wide * wide
        mean = jnp.sum(squares, axis=-1, keepdims=True) * (1.0 / 4096)
        acc = acc * lax.rsqrt(mean + 1e-05)
        cosine = jnp.concatenate([cos_ref[(y + r) & 3, span] for r in range(NY)], axis=0)
        sine = jnp.concatenate([sin_ref[(y + r) & 3, span] for r in range(NY)], axis=0)
        key = turn(acc[:, 128:256], cosine, sine).astype(BF16)
        query = (turn(acc[:, :128], cosine, sine) * QSCALE).astype(BF16)
        out_ref[:, span, :128] = key.reshape(4, 64, 128)
        out_ref[:, span, 128:256] = acc[:, 256:].astype(BF16).reshape(4, 64, 128)
        out_ref[:, span, 256:] = query.reshape(4, 64, 128)


SCALARS = pl.BlockSpec(memory_space=pltpu.SMEM)
WHOLE = pl.BlockSpec(memory_space=pltpu.VMEM)
STATE = jax.ShapeDtypeStruct((2, 4, 128, 128), F32)


def project(where, pieces, w, cosine, sine):
    return pl.pallas_call(
        project_kernel,
        in_specs=[SCALARS] + [WHOLE] * 7,
        out_specs=WHOLE,
        out_shape=jax.ShapeDtypeStruct((NY, SEL_DEV, 384), BF16),
        compiler_params=pltpu.CompilerParams(vmem_limit_bytes=40 << 20),
        cost_estimate=pl.CostEstimate(flops=2 * 512 * 4096 * 384, bytes_accessed=8 << 20, transcendentals=512),
    )(where, *pieces, w, cosine, sine)


def attend_kernel(away, where_ref, kv_ref, own_ref, twin_ref, *refs):
    ins, outs = refs[:-2], refs[-2:]
    z, y, c = where_ref[0], where_ref[1], where_ref[2]
    cores = kv_ref.shape[0]
    row = lax.broadcasted_iota(I32, (256, 1), 0)
    rank_q = row % 32 * 64 + z * 8 + ((y + row // 32) & 3) * 2 + ((c + row // 128) & 1)
    col = lax.broadcasted_iota(I32, (1, cores * 128), 1)
    from_z = (z + away * (2 * c - 1)) & 7
    rank_k = col % 32 * 64 + from_z * 8 + ((y + col // 32) & 3) * 2 + ((c + col // 128) & 1)
    seen = rank_k <= rank_q

    def block(low, high, part):
        lanes = slice(part * 128, part * 128 + 128)
        return kv_ref[:, :, low:high, lanes].reshape(cores * 4 * (high - low), 128)

    def dot_t(a, b):
        return lax.dot_general(a, b, (((1,), (1,)), ((), ())), preferred_element_type=F32)

    for t in range(4):
        low, high = t * 32, t * 32 + 32
        query = jnp.concatenate(
            [r[:, low:high, 256:].reshape(128, 128) for r in (own_ref, twin_ref)], axis=0
        )
        edge = jnp.where(seen, dot_t(query, block(low, high, 0)), NEG)
        new = jnp.max(edge, axis=-1, keepdims=True)
        if t:
            past = dot_t(query, block(0, low, 0))
            new = jnp.maximum(new, jnp.max(past, axis=-1, keepdims=True))
        if ins:
            stats = jnp.concatenate([ins[0][1, t], ins[1][1, t]], axis=0)
            old = stats[:, :1]
            new = jnp.maximum(new, old)
        weights = jnp.exp2(edge - new)
        total = jnp.sum(weights, axis=-1, keepdims=True)
        acc = jnp.dot(weights.astype(BF16), block(low, high, 1), preferred_element_type=F32)
        if t:
            weights = jnp.exp2(past - new)
            total += jnp.sum(weights, axis=-1, keepdims=True)
            acc += jnp.dot(weights.astype(BF16), block(0, low, 1), preferred_element_type=F32)
        if ins:
            shrink = jnp.exp2(old - new)
            total += stats[:, 64:65] * shrink
            acc += jnp.concatenate([ins[0][0, t], ins[1][0, t]], axis=0) * shrink
        lane = lax.broadcasted_iota(I32, (256, 128), 1)
        stats = jnp.where(lane < 64, new, total)
        for half in range(2):
            outs[half][0, t] = acc[half * 128 : half * 128 + 128]
            outs[half][1, t] = stats[half * 128 : half * 128 + 128]


def attend(where, away, kv, own, twin, states):
    keys = kv.shape[0] * 512
    return pl.pallas_call(
        functools.partial(attend_kernel, away),
        in_specs=[SCALARS] + [WHOLE] * (3 + len(states)),
        out_specs=[WHOLE, WHOLE],
        out_shape=[STATE, STATE],
        compiler_params=pltpu.CompilerParams(vmem_limit_bytes=40 << 20),
        cost_estimate=pl.CostEstimate(
            flops=4 * 1024 * keys * 128, bytes_accessed=2 << 20, transcendentals=1024 * keys
        ),
    )(where, kv, own, twin, *states)


def merge_kernel(where_ref, mine_ref, other_ref, o_ref):
    y = where_ref[1]
    for t in range(4):
        mine, other = mine_ref[1, t], other_ref[1, t]
        top = jnp.maximum(mine[:, :1], other[:, :1])
        keep, add = jnp.exp2(mine[:, :1] - top), jnp.exp2(other[:, :1] - top)
        total = mine[:, 64:65] * keep + other[:, 64:65] * add
        done = ((mine_ref[0, t] * keep + other_ref[0, t] * add) / total).astype(BF16)
        for rel in range(4):
            to = (y + rel) & 3
            for x in range(NX):
                o_ref[to, x, t * 32 : t * 32 + 32, :] = done[rel * 32 : rel * 32 + 32]


def merge(where, mine, other):
    return pl.pallas_call(
        merge_kernel,
        in_specs=[SCALARS, WHOLE, WHOLE],
        out_specs=WHOLE,
        out_shape=jax.ShapeDtypeStruct((NY, NX, SEL_DEV, 128), BF16),
        compiler_params=pltpu.CompilerParams(vmem_limit_bytes=40 << 20),
    )(where, mine, other)


def spread(piece, axis):
    return lax.all_to_all(jnp.broadcast_to(piece[None], (4,) + piece.shape), axis, split_axis=0, concat_axis=0)


def rest(stack, here, span):
    return jnp.stack([lax.dynamic_index_in_dim(stack, (here + k) & 3, 0, keepdims=False)[span] for k in (1, 2, 3)])


def onward(array):
    pairs = [(z * NC, (z + 1) % NZ * NC) for z in range(NZ)]
    pairs += [(z * NC + 1, (z - 1) % NZ * NC + 1) for z in range(NZ)]
    return lax.ppermute(array, ("z", "c"), pairs)


def after(value, *others):
    return lax.optimization_barrier((value, *others))[0]


def per_device(hidden, picked, target, norm_gain, router_weight, w_query, w_key, w_value, w_out):
    z, y, c, x = (lax.axis_index(a).astype(I32) for a in ("z", "y", "c", "x"))
    shard = (z * NY + y) * NC + c
    where = jnp.stack([z, y, c, x])

    live = target >= 0
    cell = jnp.where(live, target // SEL_DEV * BUCKET + target % BUCKET, -1)
    slots = jnp.arange(SHARDS * BUCKET, dtype=I32)
    pick_out = (cell[None, :] == slots[:, None]).astype(BF16)
    outgoing = jnp.dot(pick_out, hidden, preferred_element_type=F32).astype(BF16)
    outgoing = outgoing.reshape(SHARDS, BUCKET, -1)
    arrived = lax.all_to_all(outgoing, ("z", "y", "c"), split_axis=0, concat_axis=0, tiled=True)
    arrived = arrived.reshape(SHARDS * BUCKET, -1)
    fetch = picked // hidden.shape[0] * BUCKET + jnp.arange(SEL_DEV, dtype=I32) % BUCKET
    pick_in = (fetch[:, None] == slots[None, :]).astype(BF16)
    own_rows = jnp.dot(pick_in, arrived, preferred_element_type=F32).astype(BF16)

    gain = lax.dynamic_slice(norm_gain, (shard * 64,), (64,)).astype(F32)[:, None]
    places = jnp.concatenate([picked // 256, picked % 256, jnp.zeros((128,), I32)]).astype(BF16)
    places = jnp.concatenate([places[None], jnp.zeros((15, 384), BF16)])
    w_query, w_key, w_value = (after(w, outgoing) for w in (w_query, w_key, w_value))

    def part(head):
        cut = [w[:, head * 128 : head * 128 + 128] for w in (w_query, w_key, w_value)]
        scaled = (jnp.concatenate(cut, axis=1).astype(F32) * gain).astype(BF16)
        return jnp.concatenate([scaled, places], axis=0)

    got = lax.all_to_all(jnp.stack([part(h) for h in range(NY)]), "y", split_axis=0, concat_axis=0)
    heads = got[:, :64]
    twin = shift(heads, "c", 1, NC)
    pair = jnp.stack([jnp.where(c == 0, heads, twin), jnp.where(c == 0, twin, heads)], axis=1)
    pair = after(pair, own_rows)
    ring = [pair]
    for _ in range(3):
        ring.append(onward(ring[-1]))
    ring.append(onward(lax.dynamic_index_in_dim(ring[-1], c, 1, keepdims=False)))
    mine = jnp.stack(ring[1:4])
    other = shift(jnp.concatenate([mine.reshape(3 * 512, 384), ring[4].reshape(256, 384)]), "c", 1, NC)
    last = other[1536:].reshape(NY, 64, 384)
    last = jnp.stack([jnp.where(c == 0, ring[4], last), jnp.where(c == 0, last, ring[4])], axis=1)
    weights = jnp.concatenate(
        [pair.reshape(512, 384)]
        + [other[:1536]]
        + [last.reshape(512, 384)]
        + [mine[k].reshape(512, 384) for k in (2, 1, 0)]
    ).reshape(NZ, 512, 384)

    places = got[:, 64, :].astype(F32)
    places = places[:, :128] * 256.0 + places[:, 128:256]
    half = HEAD_DIM // 2
    freq = jnp.exp(-math.log(10000.0) * (2.0 * jnp.arange(half, dtype=F32) / HEAD_DIM))
    angle = places[..., None] * freq
    cosine, sine = jnp.cos(angle), jnp.sin(angle)
    cosine = jnp.concatenate([cosine, cosine], axis=-1)
    sine = jnp.concatenate([-sine, sine], axis=-1)

    over_x, over_y = spread(own_rows, "x"), spread(own_rows, "y")
    far_a = spread(rest(over_x, x, slice(0, 64)), "y")
    far_b = spread(rest(over_y, y, slice(64, 128)), "x")
    qkv = project(where, [over_x, over_y, far_a, far_b], weights, cosine, sine)

    gate = jax.nn.sigmoid(
        jnp.einsum("xrf,xf->r", over_x, router_weight.reshape(NX, 1024), preferred_element_type=F32)
    )

    twin = shift(qkv, "c", 1, NC)
    near = onward(jnp.stack([qkv[:, :, :256], twin[:, :, :256]]))
    state = attend(where, 0, qkv[None], qkv, twin, [])
    next1, state = lax.optimization_barrier((onward(near), state))
    state = attend(where, 1, near, qkv, twin, state)
    next2, state = lax.optimization_barrier((onward(next1), state))
    state = attend(where, 2, next1, qkv, twin, state)
    far, state = lax.optimization_barrier((onward(next2[:1]), state))
    state = attend(where, 3, next2, qkv, twin, state)
    state = attend(where, 4, far, qkv, twin, state)
    ready = merge(where, state[0], shift(state[1], "c", 1, NC))

    by_head = lax.all_to_all(ready.reshape(16, SEL_DEV, 128), ("y", "x"), split_axis=0, concat_axis=0, tiled=True)
    flat = by_head.reshape(NY, NX, SEL_DEV, 128).transpose(2, 1, 0, 3).reshape(SEL_DEV, 16 * HEAD_DIM)
    update = jnp.dot(flat, w_out, preferred_element_type=F32)
    new_rows = (own_rows.astype(F32) + gate[:, None] * update).astype(BF16)
    backward = jnp.dot(pick_in.T, new_rows, preferred_element_type=F32).astype(BF16)
    returned = lax.all_to_all(
        backward.reshape(SHARDS, BUCKET, -1), ("z", "y", "c"), split_axis=0, concat_axis=0, tiled=True
    ).reshape(SHARDS * BUCKET, -1)
    taken = jnp.dot(pick_out.T, returned, preferred_element_type=F32).astype(BF16)
    return jnp.where(live[:, None], taken, hidden)


def solution(mesh):
    cut = Mesh(mesh.devices.reshape(NZ, NY, NC, NX), ("z", "y", "c", "x"))
    seq = ("z", "y", "c")
    placed = (
        P(seq, "x"),
        P(seq),
        P(seq),
        P(),
        P(),
        P(seq, "x"),
        P(seq, "x"),
        P(seq, "x"),
        P(None, "x"),
    )
    return jax.shard_map(
        per_device, mesh=cut, in_specs=placed, out_specs=P(seq, "x"), check_vma=False
    )
```

time: 251 us -> 240 us (0.956)
  waiting for transfers between devices: 146 us -> 105 us
  starting transfers between devices: 29.3 us -> 67.6 us
  between operations: 13.3 us -> 0.48 us
  blocking collectives: 20.8 us -> 10.3 us
  local copies, waits for them, and re-layouts: 14.1 us -> 20.8 us
  Pallas kernels: 12.7 us -> 19 us
  other arithmetic: 3.54 us -> 7.66 us
    all_gather x3 -> x0, waiting for transfers between devices: 98.9 us -> none  [the longest x1 55.4 us: per_device(): lax.all_gather(own_rows, ('y', 'x'), axis=0).reshape(NY, NX, SEL_DEV, 1024)]
    all_to_all x2 -> x6, waiting for transfers between devices: 26.4 us -> 56.7 us  [the longest x4 30.2 us: spread(): lax.all_to_all(jnp.broadcast_to(piece[None], (4,) + piece.shape), axis, s...]
    ppermute x3 -> x12, starting transfers between devices: 3.47 us -> 31.1 us  [the longest x4 16.9 us: shift(): lax.ppermute(array, axis, [(i, (i + by) % size) for i in range(size)])]
    ppermute x3 -> x12, waiting for transfers between devices: 3.14 us -> 30.6 us  [the longest x8 26.6 us: onward(): return lax.ppermute(array, ('z', 'c'), pairs)]
    all_to_all x2 -> x6, starting transfers between devices: 15.7 us -> 30.9 us  [the longest x4 15.6 us: spread(): lax.all_to_all(jnp.broadcast_to(piece[None], (4,) + piece.shape), axis, s...]
    all_gather x1 -> x0, blocking collectives: 10.7 us -> none  [per_device(): all_heads = lax.all_gather(by_head, 'x', axis=0, tiled=True)]
    pallas_call x2 -> x7, Pallas kernels: 12.7 us -> 19 us  [the longest x5 12.8 us: attend(): pl.pallas_call(functools.partial(attend_kernel, away), in_specs=[SCALARS]...]
    broadcast_in_dim x0 -> x4, local copies, waits for them, and re-layouts: none -> 4.78 us  [the longest x3 4.78 us: spread(): jnp.broadcast_to(piece[None], (4,) + piece.shape)]
  transfers between devices with their start and end apart: 9 -> 19, of which waited for: 8 -> 17; matrix products, arithmetic and copies ran while one was open for 5% -> 8% of each run, Pallas kernels for 0% -> 3%
where the time goes in v2:
time: 240 us; the launch traced here: 239 us
  waiting for transfers between devices  105 us (44%)
  starting transfers between devices  67.6 us (28%)
  local copies, waits for them, and re-layouts  20.8 us (9%)
  Pallas kernels  19 us (8%)
  blocking collectives  10.3 us (4%)
  matrix products  8.32 us (3%)
  other arithmetic  7.66 us (3%)
    all_to_all x4, waiting for transfers between devices, spread(): lax.all_to_all(jnp.broadcast_to(piece[None], (4,) + piece.shape), axis, s...  30.2 us
    ppermute x8, waiting for transfers between devices, onward(): return lax.ppermute(array, ('z', 'c'), pairs)  26.6 us
    all_to_all x1, waiting for transfers between devices, per_device(): lax.all_to_all(backward.reshape(SHARDS, BUCKET, -1), ('z', 'y', 'c'), spl...  17.8 us
    ppermute x4, starting transfers between devices, shift(): lax.ppermute(array, axis, [(i, (i + by) % size) for i in range(size)])  16.9 us
    all_to_all x1, waiting for transfers between devices, per_device(): lax.all_to_all(outgoing, ('z', 'y', 'c'), split_axis=0, concat_axis=0, ti...  16 us
    all_to_all x4, starting transfers between devices, spread(): lax.all_to_all(jnp.broadcast_to(piece[None], (4,) + piece.shape), axis, s...  15.6 us
    ppermute x8, starting transfers between devices, onward(): return lax.ppermute(array, ('z', 'c'), pairs)  14.3 us
    pallas_call x5, Pallas kernels, attend(): pl.pallas_call(functools.partial(attend_kernel, away), in_specs=[SCALARS]...  12.8 us
  transfers between devices with their start and end apart: 19, of which 17 were waited for; matrix products, arithmetic and copies ran while one was open for 8% of the time, Pallas kernels for 3%

profile of v2, /device:TPU:1, one launch (start us, length us, event | category | flops | bytes accessed | tf_op | source)
XLA Modules:
  0.0 239.2 jit_solution(11485120350831507663)
XLA Ops:
  0.8 2.3 convolution_convert_fusion
  5.3 10.3 %all_to_all.40 = bf16[4,80,384]{2,1,0:T(8,128)(2,1)S(1)} all-to-all(bf16[4,80,384]{2,1,0:T(8,128)(2,1)S(1)} %pad_maximum_fusion.9), channel_id=1, replica_groups=mesh['z'=8,'y'=4,'c'=2,'x'=4] {'y'}, dimensions={0} | all-to-all | bytes 491520 | tf_op jit(solution)/shard_map/all_to_all | solution.py:217
  15.6 11.7 %all-to-all-start = ((bf16[64,4,1024]{2,1,0:T(4,128)(2,1)}), bf16[64,4,1024]{2,1,0:T(4,128)(2,1)S(1)}, u32[]{:S(2)}, u32[]{:S(2)}) async-start(bf16[64,4,1024]{2,1,0:T(4,128)(2,1)} %reshape.108), calls=%async_computation | async-start | bytes 1048576 | tf_op jit(solution)/shard_map/all_to_all | solution.py:201
  29.0 16.0 %all-to-all-done = bf16[64,4,1024]{2,1,0:T(4,128)(2,1)S(1)} async-done(((bf16[64,4,1024]{2,1,0:T(4,128)(2,1)}), bf16[64,4,1024]{2,1,0:T(4,128)(2,1)S(1)}, u32[]{:S(2)}, u32[]{:S(2)}) %all-to-all-start) | async-done | bytes 524320 | tf_op jit(solution)/shard_map/all_to_all | solution.py:201
  45.4 1.8 collective-permute-start.1
  48.3 3.5 %all-to-all-start.2 = ((bf16[4,128,1024]{2,1,0:T(8,128)(2,1)}), bf16[4,128,1024]{2,1,0:T(8,128)(2,1)S(1)}, u32[]{:S(2)}, u32[]{:S(2)}) async-start(bf16[4,128,1024]{2,1,0:T(8,128)(2,1)} %broadcast_in_dim.18), calls=%async_computation.2 | async-start | bytes 2097152 | tf_op jit(solution)/shard_map/all_to_all | solution.py:173
  52.4 2.6 %collective-permute-start.2 = (bf16[4,2,64,384]{3,2,1,0:T(8,128)(2,1)S(1)}, bf16[4,2,64,384]{3,2,1,0:T(8,128)(2,1)}, u32[]{:S(2)}, u32[]{:S(2)}) collective-permute-start(bf16[4,2,64,384]{3,2,1,0:T(8,128)(2,1)S(1)} %collective-permute-done.1), channel_id=1, source_target_pairs={{0,32},{32,64},{64,96},{96,128},{128,160},{160,192},{192,224},{224... | collective-permute-start | bytes 1179656 | tf_op jit(solution)/shard_map/ppermute | solution.py:183
  55.0 4.7 %collective-permute-done.2 = bf16[4,2,64,384]{3,2,1,0:T(8,128)(2,1)} collective-permute-done((bf16[4,2,64,384]{3,2,1,0:T(8,128)(2,1)S(1)}, bf16[4,2,64,384]{3,2,1,0:T(8,128)(2,1)}, u32[]{:S(2)}, u32[]{:S(2)}) %collective-permute-start.2) | collective-permute-done | bytes 393248 | tf_op jit(solution)/shard_map/ppermute | solution.py:183
  59.8 3.4 %collective-permute-start.3 = (bf16[4,2,64,384]{3,2,1,0:T(8,128)(2,1)}, bf16[4,2,64,384]{3,2,1,0:T(8,128)(2,1)S(1)}, u32[]{:S(2)}, u32[]{:S(2)}) collective-permute-start(bf16[4,2,64,384]{3,2,1,0:T(8,128)(2,1)} %collective-permute-done.2), channel_id=1, source_target_pairs={{0,32},{32,64},{64,96},{96,128},{128,160},{160,192},{192,224},{224... | collective-permute-start | bytes 1179656 | tf_op jit(solution)/shard_map/ppermute | solution.py:183
  63.2 3.8 %all-to-all-done.2.over_y = bf16[4,128,1024]{2,1,0:T(8,128)(2,1)S(1)} async-done(((bf16[4,128,1024]{2,1,0:T(8,128)(2,1)}), bf16[4,128,1024]{2,1,0:T(8,128)(2,1)S(1)}, u32[]{:S(2)}, u32[]{:S(2)}) %all-to-all-start.2) | async-done | bytes 1048608 | tf_op jit(solution)/shard_map/all_to_all | solution.py:173
  67.0 4.0 %all-to-all-start.1 = ((bf16[4,128,1024]{2,1,0:T(8,128)(2,1)}), bf16[4,128,1024]{2,1,0:T(8,128)(2,1)S(1)}, u32[]{:S(2)}, u32[]{:S(2)}) async-start(bf16[4,128,1024]{2,1,0:T(8,128)(2,1)} %broadcast_in_dim.18), calls=%async_computation.1 | async-start | bytes 2097152 | tf_op jit(solution)/shard_map/all_to_all | solution.py:173
  72.5 3.5 %collective-permute-done.4 = bf16[4,64,384]{2,1,0:T(8,128)(2,1)S(1)} collective-permute-done((bf16[4,64,384]{2,1,0:T(8,128)(2,1)S(1)}, bf16[4,64,384]{2,1,0:T(8,128)(2,1)S(1)}, u32[]{:S(2)}, u32[]{:S(2)}) %collective-permute-start.4) | collective-permute-done | bytes 196640 | tf_op jit(solution)/shard_map/ppermute | solution.py:183
  77.2 4.1 %collective-permute-start.5 = (bf16[1792,384]{1,0:T(8,128)(2,1)}, bf16[1792,384]{1,0:T(8,128)(2,1)}, u32[]{:S(2)}, u32[]{:S(2)}) collective-permute-start(bf16[1792,384]{1,0:T(8,128)(2,1)} %pad_maximum_fusion), channel_id=1, source_target_pairs={{0,4},{4,0},{1,5},{5,1},{2,6},{6,2},{3,7},{7,3},{8,12},{12,8},{9,1... | collective-permute-start | bytes 4128776 | tf_op jit(solution)/shard_map/ppermute | solution.py:22
  81.4 3.6 %all-to-all-done.1.over_x = bf16[4,128,1024]{2,1,0:T(8,128)(2,1)S(1)} async-done(((bf16[4,128,1024]{2,1,0:T(8,128)(2,1)}), bf16[4,128,1024]{2,1,0:T(8,128)(2,1)S(1)}, u32[]{:S(2)}, u32[]{:S(2)}) %all-to-all-start.1) | async-done | bytes 1048608 | tf_op jit(solution)/shard_map/all_to_all | solution.py:173
  85.0 1.3 broadcast_in_dim.20
  86.3 3.6 %all-to-all-start.4 = ((bf16[4,3,64,1024]{3,2,1,0:T(8,128)(2,1)}), bf16[4,3,64,1024]{3,2,1,0:T(8,128)(2,1)S(1)}, u32[]{:S(2)}, u32[]{:S(2)}) async-start(bf16[4,3,64,1024]{3,2,1,0:T(8,128)(2,1)} %broadcast_in_dim.20), calls=%async_computation.4 | async-start | bytes 3145728 | tf_op jit(solution)/shard_map/all_to_all | solution.py:173
  91.2 1.8 constant_dynamic-update-slice_fusion.4
  93.9 1.6 slice.116
  95.5 13.0 %all-to-all-done.4.far_b = bf16[4,3,64,1024]{3,2,1,0:T(8,128)(2,1)S(1)} async-done(((bf16[4,3,64,1024]{3,2,1,0:T(8,128)(2,1)}), bf16[4,3,64,1024]{3,2,1,0:T(8,128)(2,1)S(1)}, u32[]{:S(2)}, u32[]{:S(2)}) %all-to-all-start.4) | async-done | bytes 1572896 | tf_op jit(solution)/shard_map/all_to_all | solution.py:173
  108.5 2.3 broadcast_in_dim.19
  110.9 4.5 %all-to-all-start.3 = ((bf16[4,3,64,1024]{3,2,1,0:T(8,128)(2,1)}), bf16[4,3,64,1024]{3,2,1,0:T(8,128)(2,1)}, u32[]{:S(2)}, u32[]{:S(2)}) async-start(bf16[4,3,64,1024]{3,2,1,0:T(8,128)(2,1)} %broadcast_in_dim.19), calls=%async_computation.3 | async-start | bytes 3145728 | tf_op jit(solution)/shard_map/all_to_all | solution.py:173
  116.6 2.5 %slice_dynamic-update-slice_fusion = bf16[4096,384]{1,0:T(8,128)(2,1)} fusion(bf16[4096,384]{1,0:T(8,128)(2,1)} %constant_dynamic-update-slice_fusion.4, bf16[1792,384]{1,0:T(8,128)(2,1)} %collective-permute-done.5), kind=kLoop, calls=%fused_computation.8 | loop fusion | bytes 2359296
  120.6 1.8 constant_dynamic-update-slice_fusion.1
  123.2 9.8 %all-to-all-done.3.far_a = bf16[4,3,64,1024]{3,2,1,0:T(8,128)(2,1)} async-done(((bf16[4,3,64,1024]{3,2,1,0:T(8,128)(2,1)}), bf16[4,3,64,1024]{3,2,1,0:T(8,128)(2,1)}, u32[]{:S(2)}, u32[]{:S(2)}) %all-to-all-start.3) | async-done | bytes 1572896 | tf_op jit(solution)/shard_map/all_to_all | solution.py:173
  133.1 1.2 copy-done.1
  134.3 1.9 copy-done.2
  136.2 4.2 %shard_map.91.own_ref = bf16[4,128,384]{2,1,0:T(8,128)(2,1)S(1)} custom-call(s32[4]{0:T(128)S(1)} %pad_add_fusion.where_ref, bf16[4,128,1024]{2,1,0:T(8,128)(2,1)S(1)} %all-to-all-done.1.over_x, bf16[4,128,1024]{2,1,0:T(8,128)(2,1)S(1)} %copy-done.1, bf16[4,3,64,1024]{3,2,1,0:T(8,128)(2,1)} %all-to-all-done.3.far_a, ...), custom_call_target="tpu_custom_call" | custom-call | flops 1610612736 | bytes 8388608 | tf_op jit(solution)/shard_map/pallas_call | solution.py:74
  140.4 4.0 %collective-permute-start.6 = (bf16[4,128,384]{2,1,0:T(8,128)(2,1)S(1)}, bf16[4,128,384]{2,1,0:T(8,128)(2,1)S(1)}, u32[]{:S(2)}, u32[]{:S(2)}) collective-permute-start(bf16[4,128,384]{2,1,0:T(8,128)(2,1)S(1)} %shard_map.91.own_ref), channel_id=1, source_target_pairs={{0,4},{4,0},{1,5},{5,1},{2,6},{6,2},{3,7},{7,3},{8,12},{12,8},{9,1... | collective-permute-start | bytes 1179656 | tf_op jit(solution)/shard_map/ppermute | solution.py:22
  144.4 1.3 collective-permute-done.6.twin_ref
  145.9 8.3 %collective-permute-done.7.kv_ref = bf16[2,4,128,256]{3,2,1,0:T(8,128)(2,1)S(1)} collective-permute-done((bf16[2,4,128,256]{3,2,1,0:T(8,128)(2,1)S(1)}, bf16[2,4,128,256]{3,2,1,0:T(8,128)(2,1)S(1)}, u32[]{:S(2)}, u32[]{:S(2)}) %collective-permute-start.7) | collective-permute-done | bytes 524320 | tf_op jit(solution)/shard_map/ppermute | solution.py:183
  155.1 1.6 shard_map.92
  156.7 5.8 %collective-permute-done.8.kv_ref = bf16[2,4,128,256]{3,2,1,0:T(8,128)(2,1)S(1)} collective-permute-done((bf16[2,4,128,256]{3,2,1,0:T(8,128)(2,1)S(1)}, bf16[2,4,128,256]{3,2,1,0:T(8,128)(2,1)S(1)}, u32[]{:S(2)}, u32[]{:S(2)}) %collective-permute-start.8) | collective-permute-done | bytes 524320 | tf_op jit(solution)/shard_map/ppermute | solution.py:183
  162.5 1.8 collective-permute-start.9
  164.3 2.9 %shard_map.93 = (f32[2,4,128,128]{3,2,1,0:T(8,128)S(1)}, f32[2,4,128,128]{3,2,1,0:T(8,128)S(1)}) custom-call(s32[4]{0:T(128)S(1)} %pad_add_fusion.where_ref, bf16[2,4,128,256]{3,2,1,0:T(8,128)(2,1)S(1)} %collective-permute-done.7.kv_ref, bf16[4,128,384]{2,1,0:T(8,128)(2,1)S(1)} %shard_map.91.own_ref, ...), custom_call_target="tpu_custom_call" | custom-call | flops 536870912 | bytes 2097152 | tf_op jit(solution)/shard_map/pallas_call | solution.py:136
  167.2 3.3 %collective-permute-done.9.kv_ref = bf16[2,4,128,256]{3,2,1,0:T(8,128)(2,1)S(1)} collective-permute-done((bf16[2,4,128,256]{3,2,1,0:T(8,128)(2,1)S(1)}, bf16[2,4,128,256]{3,2,1,0:T(8,128)(2,1)S(1)}, u32[]{:S(2)}, u32[]{:S(2)}) %collective-permute-start.9) | collective-permute-done | bytes 524320 | tf_op jit(solution)/shard_map/ppermute | solution.py:183
  170.6 3.3 %collective-permute-start.10 = (bf16[1,4,128,256]{3,2,1,0:T(8,128)(2,1)S(1)}, bf16[1,4,128,256]{3,2,1,0:T(8,128)(2,1)S(1)}, u32[]{:S(2)}, u32[]{:S(2)}) collective-permute-start(bf16[1,4,128,256]{3,2,1,0:T(8,128)(2,1)S(1)} %slice.113), channel_id=1, source_target_pairs={{0,32},{32,64},{64,96},{96,128},{128,160},{160,192},{192,224},{224... | collective-permute-start | bytes 786440 | tf_op jit(solution)/shard_map/ppermute | solution.py:183
  173.9 2.9 %shard_map.94 = (f32[2,4,128,128]{3,2,1,0:T(8,128)S(1)}, f32[2,4,128,128]{3,2,1,0:T(8,128)S(1)}) custom-call(s32[4]{0:T(128)S(1)} %pad_add_fusion.where_ref, bf16[2,4,128,256]{3,2,1,0:T(8,128)(2,1)S(1)} %collective-permute-done.8.kv_ref, bf16[4,128,384]{2,1,0:T(8,128)(2,1)S(1)} %shard_map.91.own_ref, ...), custom_call_target="tpu_custom_call" | custom-call | flops 536870912 | bytes 2097152 | tf_op jit(solution)/shard_map/pallas_call | solution.py:136
  177.2 2.9 %shard_map.95 = (f32[2,4,128,128]{3,2,1,0:T(8,128)S(1)}, f32[2,4,128,128]{3,2,1,0:T(8,128)S(1)}) custom-call(s32[4]{0:T(128)S(1)} %pad_add_fusion.where_ref, bf16[2,4,128,256]{3,2,1,0:T(8,128)(2,1)S(1)} %collective-permute-done.9.kv_ref, bf16[4,128,384]{2,1,0:T(8,128)(2,1)S(1)} %shard_map.91.own_ref, ...), custom_call_target="tpu_custom_call" | custom-call | flops 536870912 | bytes 2097152 | tf_op jit(solution)/shard_map/pallas_call | solution.py:136
  180.1 2.6 %shard_map.96 = (f32[2,4,128,128]{3,2,1,0:T(8,128)S(1)}, f32[2,4,128,128]{3,2,1,0:T(8,128)S(1)}) custom-call(s32[4]{0:T(128)S(1)} %pad_add_fusion.where_ref, bf16[1,4,128,256]{3,2,1,0:T(8,128)(2,1)S(1)} %collective-permute-done.10.kv_ref, bf16[4,128,384]{2,1,0:T(8,128)(2,1)S(1)} %shard_map.91.own_ref, ...), custom_call_target="tpu_custom_call" | custom-call | flops 268435456 | bytes 2097152 | tf_op jit(solution)/shard_map/pallas_call | solution.py:136
  182.8 8.2 %collective-permute-start.11 = (f32[2,4,128,128]{3,2,1,0:T(8,128)S(1)}, f32[2,4,128,128]{3,2,1,0:T(8,128)S(1)}, u32[]{:S(2)}, u32[]{:S(2)}) collective-permute-start(f32[2,4,128,128]{3,2,1,0:T(8,128)S(1)} %get-tuple-element.50), channel_id=1, source_target_pairs={{0,4},{4,0},{1,5},{5,1},{2,6},{6,2},{3,7},{7,3},{8,12},{12,8},{9,1... | collective-permute-start | bytes 1572872 | tf_op jit(solution)/shard_map/ppermute | solution.py:22
  190.9 1.5 collective-permute-done.11.other_ref
  192.5 2.0 shard_map.97
  194.4 3.6 %all-to-all-start.6 = ((bf16[16,128,128]{2,1,0:T(8,128)(2,1)}), bf16[16,128,128]{2,1,0:T(8,128)(2,1)S(1)}, u32[]{:S(2)}, u32[]{:S(2)}) async-start(bf16[16,128,128]{2,1,0:T(8,128)(2,1)} %bitcast.32), calls=%async_computation.6 | async-start | bytes 1048576 | tf_op jit(solution)/shard_map/all_to_all | solution.py:267
  198.4 10.6 %all-to-all-done.6 = bf16[16,128,128]{2,1,0:T(8,128)(2,1)S(1)} async-done(((bf16[16,128,128]{2,1,0:T(8,128)(2,1)}), bf16[16,128,128]{2,1,0:T(8,128)(2,1)S(1)}, u32[]{:S(2)}, u32[]{:S(2)}) %all-to-all-start.6) | async-done | bytes 524320 | tf_op jit(solution)/shard_map/all_to_all | solution.py:267
  209.3 3.2 %convolution_convert_fusion.1 = bf16[256,1024]{1,0:T(8,128)(2,1)S(1)} fusion(bf16[128,2048]{0,1:T(8,128)(2,1)S(1)} %bitcast.75, bf16[2048,1024]{1,0:T(8,128)(2,1)} %param.17, bf16[128,1024]{1,0:T(8,128)(2,1)S(1)} %copy-done.4, f32[128]{0:T(128)S(1)} %fusion.5, s32[128]{0:T(128)S(1)} %get-tuple-element.85), kind=kOutput, calls=%fused_computation.3 | convolution fusion | flops 604798976 | bytes 5506048 | tf_op jit(solution)/shard_map/dot_general | solution.py:271
  213.5 5.6 %all-to-all-start.7 = ((bf16[64,4,1024]{2,1,0:T(4,128)(2,1)}), bf16[64,4,1024]{2,1,0:T(4,128)(2,1)S(1)}, u32[]{:S(2)}, u32[]{:S(2)}) async-start(bf16[64,4,1024]{2,1,0:T(4,128)(2,1)} %reshape.120), calls=%async_computation.7 | async-start | bytes 1048576 | tf_op jit(solution)/shard_map/all_to_all | solution.py:272
  219.1 17.8 %all-to-all-done.7 = bf16[64,4,1024]{2,1,0:T(4,128)(2,1)S(1)} async-done(((bf16[64,4,1024]{2,1,0:T(4,128)(2,1)}), bf16[64,4,1024]{2,1,0:T(4,128)(2,1)S(1)}, u32[]{:S(2)}, u32[]{:S(2)}) %all-to-all-start.7) | async-done | bytes 524320 | tf_op jit(solution)/shard_map/all_to_all | solution.py:272
  237.0 2.2 convert_select_fusion
  (88 shorter events, 18.5 us)
Async XLA Ops:
  0.0 4.9 %copy-start.10 = (bf16[64,512]{1,0:T(8,128)(2,1)S(1)}, bf16[64,512]{1,0:T(8,128)(2,1)}, u32[]{:S(2)}) copy-start(bf16[64,512]{1,0:T(8,128)(2,1)} %param.14) | copy-start | bytes 196612
  0.0 4.9 %copy-start.11 = (bf16[64,512]{1,0:T(8,128)(2,1)S(1)}, bf16[64,512]{1,0:T(8,128)(2,1)}, u32[]{:S(2)}) copy-start(bf16[64,512]{1,0:T(8,128)(2,1)} %param.15) | copy-start | bytes 196612
  0.0 4.1 %copy-start.9 = (bf16[64,512]{1,0:T(8,128)(2,1)S(1)}, bf16[64,512]{1,0:T(8,128)(2,1)}, u32[]{:S(2)}) copy-start(bf16[64,512]{1,0:T(8,128)(2,1)} %param.16) | copy-start | bytes 196612
  0.0 4.1 %copy-start.14 = (s32[128]{0:T(128)S(1)}, s32[128]{0:T(128)}, u32[]{:S(2)}) copy-start(s32[128]{0:T(128)} %param.10) | copy-start | bytes 1540
  15.6 29.4 %all-to-all-start = ((bf16[64,4,1024]{2,1,0:T(4,128)(2,1)}), bf16[64,4,1024]{2,1,0:T(4,128)(2,1)S(1)}, u32[]{:S(2)}, u32[]{:S(2)}) async-start(bf16[64,4,1024]{2,1,0:T(4,128)(2,1)} %reshape.108), calls=%async_computation | async-start | bytes 1048576 | tf_op jit(solution)/shard_map/all_to_all | solution.py:201
  27.3 1.6 collective-permute-start
  29.0 26.0 %copy-start.7 = (bf16[4,2,64,384]{3,2,1,0:T(8,128)(2,1)}, bf16[4,2,64,384]{3,2,1,0:T(8,128)(2,1)S(1)}, u32[]{:S(2)}) copy-start(bf16[4,2,64,384]{3,2,1,0:T(8,128)(2,1)S(1)} %pad_maximum_fusion.5) | copy-start | bytes 1179652
  45.4 21.6 %copy-start.3 = (bf16[128,1024]{1,0:T(8,128)(2,1)}, bf16[128,1024]{1,0:T(8,128)(2,1)S(1)}, u32[]{:S(2)}) copy-start(bf16[128,1024]{1,0:T(8,128)(2,1)S(1)} %convolution_convert_fusion.2) | copy-start | bytes 786436
  45.4 7.0 %collective-permute-start.1 = (bf16[4,2,64,384]{3,2,1,0:T(8,128)(2,1)S(1)}, bf16[4,2,64,384]{3,2,1,0:T(8,128)(2,1)S(1)}, u32[]{:S(2)}, u32[]{:S(2)}) collective-permute-start(bf16[4,2,64,384]{3,2,1,0:T(8,128)(2,1)S(1)} %pad_maximum_fusion.5), channel_id=1, source_target_pairs={{0,32},{32,64},{64,96},{96,128},{128,160},{160,192},{192,224},{224... | collective-permute-start | bytes 1179656 | tf_op jit(solution)/shard_map/ppermute | solution.py:183
  48.3 18.7 %all-to-all-start.2 = ((bf16[4,128,1024]{2,1,0:T(8,128)(2,1)}), bf16[4,128,1024]{2,1,0:T(8,128)(2,1)S(1)}, u32[]{:S(2)}, u32[]{:S(2)}) async-start(bf16[4,128,1024]{2,1,0:T(8,128)(2,1)} %broadcast_in_dim.18), calls=%async_computation.2 | async-start | bytes 2097152 | tf_op jit(solution)/shard_map/all_to_all | solution.py:173
  52.4 20.1 %copy-start.5 = (bf16[4,2,64,384]{3,2,1,0:T(8,128)(2,1)}, bf16[4,2,64,384]{3,2,1,0:T(8,128)(2,1)S(1)}, u32[]{:S(2)}) copy-start(bf16[4,2,64,384]{3,2,1,0:T(8,128)(2,1)S(1)} %collective-permute-done.1) | copy-start | bytes 1179652
  52.4 7.4 %collective-permute-start.2 = (bf16[4,2,64,384]{3,2,1,0:T(8,128)(2,1)S(1)}, bf16[4,2,64,384]{3,2,1,0:T(8,128)(2,1)}, u32[]{:S(2)}, u32[]{:S(2)}) collective-permute-start(bf16[4,2,64,384]{3,2,1,0:T(8,128)(2,1)S(1)} %collective-permute-done.1), channel_id=1, source_target_pairs={{0,32},{32,64},{64,96},{96,128},{128,160},{160,192},{192,224},{224... | collective-permute-start | bytes 1179656 | tf_op jit(solution)/shard_map/ppermute | solution.py:183
  59.8 11.3 %collective-permute-start.3 = (bf16[4,2,64,384]{3,2,1,0:T(8,128)(2,1)}, bf16[4,2,64,384]{3,2,1,0:T(8,128)(2,1)S(1)}, u32[]{:S(2)}, u32[]{:S(2)}) collective-permute-start(bf16[4,2,64,384]{3,2,1,0:T(8,128)(2,1)} %collective-permute-done.2), channel_id=1, source_target_pairs={{0,32},{32,64},{64,96},{96,128},{128,160},{160,192},{192,224},{224... | collective-permute-start | bytes 1179656 | tf_op jit(solution)/shard_map/ppermute | solution.py:183
  67.0 5.5 %copy-start = (bf16[4,128,1024]{2,1,0:T(8,128)(2,1)}, bf16[4,128,1024]{2,1,0:T(8,128)(2,1)S(1)}, u32[]{:S(2)}) copy-start(bf16[4,128,1024]{2,1,0:T(8,128)(2,1)S(1)} %all-to-all-done.2.over_y) | copy-start | bytes 3145732
  67.0 18.0 %all-to-all-start.1 = ((bf16[4,128,1024]{2,1,0:T(8,128)(2,1)}), bf16[4,128,1024]{2,1,0:T(8,128)(2,1)S(1)}, u32[]{:S(2)}, u32[]{:S(2)}) async-start(bf16[4,128,1024]{2,1,0:T(8,128)(2,1)} %broadcast_in_dim.18), calls=%async_computation.1 | async-start | bytes 2097152 | tf_op jit(solution)/shard_map/all_to_all | solution.py:173
  71.1 4.9 %collective-permute-start.4 = (bf16[4,64,384]{2,1,0:T(8,128)(2,1)S(1)}, bf16[4,64,384]{2,1,0:T(8,128)(2,1)S(1)}, u32[]{:S(2)}, u32[]{:S(2)}) collective-permute-start(bf16[4,64,384]{2,1,0:T(8,128)(2,1)S(1)} %dynamic-slice_bitcast_fusion), channel_id=1, source_target_pairs={{0,32},{32,64},{64,96},{96,128},{128,160},{160,192},{192,224},{224... | collective-permute-start | bytes 589832 | tf_op jit(solution)/shard_map/ppermute | solution.py:183
  76.0 10.3 %copy-start.8 = (bf16[4,64,384]{2,1,0:T(8,128)(2,1)}, bf16[4,64,384]{2,1,0:T(8,128)(2,1)S(1)}, u32[]{:S(2)}) copy-start(bf16[4,64,384]{2,1,0:T(8,128)(2,1)S(1)} %collective-permute-done.4) | copy-start | bytes 589828
  77.2 16.7 %collective-permute-start.5 = (bf16[1792,384]{1,0:T(8,128)(2,1)}, bf16[1792,384]{1,0:T(8,128)(2,1)}, u32[]{:S(2)}, u32[]{:S(2)}) collective-permute-start(bf16[1792,384]{1,0:T(8,128)(2,1)} %pad_maximum_fusion), channel_id=1, source_target_pairs={{0,4},{4,0},{1,5},{5,1},{2,6},{6,2},{3,7},{7,3},{8,12},{12,8},{9,1... | collective-permute-start | bytes 4128776 | tf_op jit(solution)/shard_map/ppermute | solution.py:22
  86.3 22.2 %all-to-all-start.4 = ((bf16[4,3,64,1024]{3,2,1,0:T(8,128)(2,1)}), bf16[4,3,64,1024]{3,2,1,0:T(8,128)(2,1)S(1)}, u32[]{:S(2)}, u32[]{:S(2)}) async-start(bf16[4,3,64,1024]{3,2,1,0:T(8,128)(2,1)} %broadcast_in_dim.20), calls=%async_computation.4 | async-start | bytes 3145728 | tf_op jit(solution)/shard_map/all_to_all | solution.py:173
  110.9 22.2 %all-to-all-start.3 = ((bf16[4,3,64,1024]{3,2,1,0:T(8,128)(2,1)}), bf16[4,3,64,1024]{3,2,1,0:T(8,128)(2,1)}, u32[]{:S(2)}, u32[]{:S(2)}) async-start(bf16[4,3,64,1024]{3,2,1,0:T(8,128)(2,1)} %broadcast_in_dim.19), calls=%async_computation.3 | async-start | bytes 3145728 | tf_op jit(solution)/shard_map/all_to_all | solution.py:173
  116.5 5.9 %copy-start.6 = (bf16[4,2,64,384]{3,2,1,0:T(8,128)(2,1)S(1)}, bf16[4,2,64,384]{3,2,1,0:T(8,128)(2,1)}, u32[]{:S(2)}) copy-start(bf16[4,2,64,384]{3,2,1,0:T(8,128)(2,1)} %copy-done.5) | copy-start | bytes 1179652
  133.1 1.2 copy-start.1
  134.3 1.9 copy-start.2
  140.4 5.3 %collective-permute-start.6 = (bf16[4,128,384]{2,1,0:T(8,128)(2,1)S(1)}, bf16[4,128,384]{2,1,0:T(8,128)(2,1)S(1)}, u32[]{:S(2)}, u32[]{:S(2)}) collective-permute-start(bf16[4,128,384]{2,1,0:T(8,128)(2,1)S(1)} %shard_map.91.own_ref), channel_id=1, source_target_pairs={{0,4},{4,0},{1,5},{5,1},{2,6},{6,2},{3,7},{7,3},{8,12},{12,8},{9,1... | collective-permute-start | bytes 1179656 | tf_op jit(solution)/shard_map/ppermute | solution.py:22
  145.8 8.4 %collective-permute-start.7 = (bf16[2,4,128,256]{3,2,1,0:T(8,128)(2,1)S(1)}, bf16[2,4,128,256]{3,2,1,0:T(8,128)(2,1)S(1)}, u32[]{:S(2)}, u32[]{:S(2)}) collective-permute-start(bf16[2,4,128,256]{3,2,1,0:T(8,128)(2,1)S(1)} %pad_maximum_fusion.2), channel_id=1, source_target_pairs={{0,32},{32,64},{64,96},{96,128},{128,160},{160,192},{192,224},{224... | collective-permute-start | bytes 1572872 | tf_op jit(solution)/shard_map/ppermute | solution.py:183
  154.2 8.3 %collective-permute-start.8 = (bf16[2,4,128,256]{3,2,1,0:T(8,128)(2,1)S(1)}, bf16[2,4,128,256]{3,2,1,0:T(8,128)(2,1)S(1)}, u32[]{:S(2)}, u32[]{:S(2)}) collective-permute-start(bf16[2,4,128,256]{3,2,1,0:T(8,128)(2,1)S(1)} %collective-permute-done.7.kv_ref), channel_id=1, source_target_pairs={{0,32},{32,64},{64,96},{96,128},{128,160},{160,192},{192,224},{224... | collective-permute-start | bytes 1572872 | tf_op jit(solution)/shard_map/ppermute | solution.py:183
  162.5 8.0 %collective-permute-start.9 = (bf16[2,4,128,256]{3,2,1,0:T(8,128)(2,1)S(1)}, bf16[2,4,128,256]{3,2,1,0:T(8,128)(2,1)S(1)}, u32[]{:S(2)}, u32[]{:S(2)}) collective-permute-start(bf16[2,4,128,256]{3,2,1,0:T(8,128)(2,1)S(1)} %collective-permute-done.8.kv_ref), channel_id=1, source_target_pairs={{0,32},{32,64},{64,96},{96,128},{128,160},{160,192},{192,224},{224... | collective-permute-start | bytes 1572872 | tf_op jit(solution)/shard_map/ppermute | solution.py:183
  170.6 6.7 %collective-permute-start.10 = (bf16[1,4,128,256]{3,2,1,0:T(8,128)(2,1)S(1)}, bf16[1,4,128,256]{3,2,1,0:T(8,128)(2,1)S(1)}, u32[]{:S(2)}, u32[]{:S(2)}) collective-permute-start(bf16[1,4,128,256]{3,2,1,0:T(8,128)(2,1)S(1)} %slice.113), channel_id=1, source_target_pairs={{0,32},{32,64},{64,96},{96,128},{128,160},{160,192},{192,224},{224... | collective-permute-start | bytes 786440 | tf_op jit(solution)/shard_map/ppermute | solution.py:183
  180.1 17.9 %copy-start.13 = (bf16[4096]{0:T(1024)(128)(2,1)S(1)}, bf16[4096]{0:T(1024)(128)(2,1)}, u32[]{:S(2)}) copy-start(bf16[4096]{0:T(1024)(128)(2,1)} %param.13) | copy-start | bytes 24580
  182.7 26.5 %copy-start.4 = (bf16[128,1024]{1,0:T(8,128)(2,1)S(1)}, bf16[128,1024]{1,0:T(8,128)(2,1)}, u32[]{:S(2)}) copy-start(bf16[128,1024]{1,0:T(8,128)(2,1)} %copy-done.3) | copy-start | bytes 786436
  182.8 9.7 %collective-permute-start.11 = (f32[2,4,128,128]{3,2,1,0:T(8,128)S(1)}, f32[2,4,128,128]{3,2,1,0:T(8,128)S(1)}, u32[]{:S(2)}, u32[]{:S(2)}) collective-permute-start(f32[2,4,128,128]{3,2,1,0:T(8,128)S(1)} %get-tuple-element.50), channel_id=1, source_target_pairs={{0,4},{4,0},{1,5},{5,1},{2,6},{6,2},{3,7},{7,3},{8,12},{12,8},{9,1... | collective-permute-start | bytes 1572872 | tf_op jit(solution)/shard_map/ppermute | solution.py:22
  194.4 14.5 %all-to-all-start.6 = ((bf16[16,128,128]{2,1,0:T(8,128)(2,1)}), bf16[16,128,128]{2,1,0:T(8,128)(2,1)S(1)}, u32[]{:S(2)}, u32[]{:S(2)}) async-start(bf16[16,128,128]{2,1,0:T(8,128)(2,1)} %bitcast.32), calls=%async_computation.6 | async-start | bytes 1048576 | tf_op jit(solution)/shard_map/all_to_all | solution.py:267
  209.3 9.8 %copy-start.12 = (s32[1024]{0:T(1024)S(1)}, s32[1024]{0:T(1024)}, u32[]{:S(2)}) copy-start(s32[1024]{0:T(1024)} %param.11) | copy-start | bytes 12292
  212.5 24.5 %copy-start.15 = (bf16[1024,1024]{1,0:T(8,128)(2,1)S(1)}, bf16[1024,1024]{1,0:T(8,128)(2,1)}, u32[]{:S(2)}) copy-start(bf16[1024,1024]{1,0:T(8,128)(2,1)} %param.9) | copy-start | bytes 6291460
  213.5 23.4 %all-to-all-start.7 = ((bf16[64,4,1024]{2,1,0:T(4,128)(2,1)}), bf16[64,4,1024]{2,1,0:T(4,128)(2,1)S(1)}, u32[]{:S(2)}, u32[]{:S(2)}) async-start(bf16[64,4,1024]{2,1,0:T(4,128)(2,1)} %reshape.120), calls=%async_computation.7 | async-start | bytes 1048576 | tf_op jit(solution)/shard_map/all_to_all | solution.py:272
